TPU v7x, 128 devices: a whole 4x4x4 slice. The times are simulated.
128 devices in a mesh: section: 16 (over z, x), dp: 8 (over y, core).
Axes of the slice: x: 4, y: 4, z: 4, core: 2. Of those that a mesh axis runs over, the one named last changes fastest.
Arguments:
- cotangent: bfloat16 [4, 128, 6144], P(None, 'dp'), may hold values from -6 to 6
- saved_inputs: bfloat16 [2, 16, 4, 128, 6144], P(None, 'section', None, 'dp'), may hold values from -6 to 6
- weights: bfloat16 [2, 16, 3072, 6144], P(None, 'section', 'dp'), may hold values from -0.0546875 to 0.0546875
Outputs:
- section_grads: bfloat16 [16, 4, 128, 6144], P('section', None, 'dp')
- weight_grads: bfloat16 [2, 16, 3072, 6144], P(None, 'section', 'dp')
- grad_peak: float32 [], replicated
All inputs are finite; a program needn't handle non-finite values.
Results may differ from a plain program's by a relative error of at most 0.039.
Values may be sent and summed in bfloat16 or wider, within the bound.
A program may use at most 128 MiB of HBM per device.

v0:
```python
import jax
import jax.numpy as jnp
from jax import lax
from jax.sharding import PartitionSpec as P

epsilon = 1e-05


def passed_along(value, axis, by):
    length = lax.axis_size(axis)
    pairs = [(i, i + by) for i in range(length) if 0 <= i + by < length]
    return lax.ppermute(value, axis, pairs)


def norm_parts(inputs):
    values = inputs.astype(jnp.float32)
    scale = lax.rsqrt(jnp.mean(values * values, axis=-1, keepdims=True) + epsilon)
    normed = values * scale
    half = normed.shape[-1] // 2
    first = normed[..., :half]
    gated = jax.nn.sigmoid(normed[..., half:])
    return (normed, scale, first, gated)


def input_grad(cot_in, inputs, head_grad):
    normed, scale, first, gated = norm_parts(inputs)
    norm_grad = jnp.concatenate(
        [head_grad * gated, head_grad * first * gated * (1.0 - gated)], axis=-1
    )
    result = cot_in.astype(jnp.float32) + scale * (
        norm_grad - normed * jnp.mean(norm_grad * normed, axis=-1, keepdims=True)
    )
    return result.astype(jnp.bfloat16)


def backward_pass(cot_in, inputs, rows):
    gathered = lax.all_gather(cot_in, "dp", axis=0, tiled=True)
    partial_grad = lax.dot_general(
        gathered, rows, (((1,), (1,)), ((), ())), preferred_element_type=jnp.float32
    )
    head_grad = lax.all_to_all(partial_grad, "dp", split_axis=0, concat_axis=1, tiled=True)
    return (input_grad(cot_in, inputs, head_grad), gathered)


def run_leg(rows, activations, lag_count, entry_values, is_entry, sender):
    batches = activations.shape[0]
    tok_count = activations.shape[1]
    width = activations.shape[2]
    replicas = lax.axis_size("dp")
    outputs = jnp.zeros((batches, tok_count, width), jnp.bfloat16)
    stashed = jnp.zeros((batches, replicas * tok_count, width), jnp.bfloat16)

    def advance(position, carry):
        incoming, outputs, stashed = carry
        which_batch = position - lag_count
        active_now = jnp.logical_and(which_batch >= 0, which_batch < batches)
        batch_index = jnp.clip(which_batch, 0, batches - 1)
        arriving = jnp.where(
            is_entry, lax.dynamic_index_in_dim(entry_values, batch_index, 0, False), incoming
        )
        inputs_now = lax.dynamic_index_in_dim(activations, batch_index, 0, False)
        leaving, gathered = backward_pass(arriving, inputs_now, rows)
        updated_outputs = lax.dynamic_update_index_in_dim(outputs, leaving, batch_index, 0)
        updated_stashed = lax.dynamic_update_index_in_dim(stashed, gathered, batch_index, 0)
        outputs = jnp.where(active_now, updated_outputs, outputs)
        stashed = jnp.where(active_now, updated_stashed, stashed)
        leaving = jnp.where(active_now, leaving, jnp.zeros_like(leaving))
        return (sender(leaving), outputs, stashed)

    start_carry = (jnp.zeros((tok_count, width), jnp.bfloat16), outputs, stashed)
    final_carry = lax.fori_loop(0, lax.axis_size("section") + batches - 1, advance, start_carry)
    return (final_carry[1], final_carry[2])


def weight_grad(stashed, activations):
    normed, scale, first, gated = norm_parts(activations)
    feats = (first * gated).astype(jnp.bfloat16)
    columns = lax.all_to_all(feats, "dp", split_axis=2, concat_axis=1, tiled=True)
    width = activations.shape[2]
    flat_cols = columns.reshape(-1, columns.shape[-1])
    flat_cots = stashed.reshape(-1, width)
    return lax.dot_general(
        flat_cols, flat_cots, (((0,), (0,)), ((), ())), preferred_element_type=jnp.float32
    )


def on_device(cotangent, saved_inputs, weights):
    section_index = lax.axis_index("section")
    section_count = lax.axis_size("section")
    acts_up = saved_inputs[0, 0]
    acts_down = saved_inputs[1, 0]
    rows_up = weights[0, 0]
    rows_down = weights[1, 0]

    def send_down(values):
        return passed_along(values, "section", 1)

    def send_up(values):
        return passed_along(values, "section", -1)

    outs_down, stash_down = run_leg(
        rows_down, acts_down, section_index, cotangent, section_index == 0, send_down
    )
    outs_up, stash_up = run_leg(
        rows_up,
        acts_up,
        section_count - 1 - section_index,
        outs_down,
        section_index == section_count - 1,
        send_up,
    )
    grad_down = weight_grad(stash_down, acts_down)
    grad_up = weight_grad(stash_up, acts_up)
    local_sum = jnp.sum(grad_up * grad_up) + jnp.sum(grad_down * grad_down)
    local_top = jnp.maximum(jnp.max(jnp.abs(grad_up)), jnp.max(jnp.abs(grad_down)))
    total = lax.psum(local_sum, ("section", "dp"))
    largest = lax.pmax(local_top, ("section", "dp"))
    width = acts_up.shape[-1]
    limit = 0.5 * jnp.sqrt(jnp.float32(2 * section_count * (width // 2) * width))
    factor = jnp.minimum(jnp.float32(1.0), limit / jnp.sqrt(total))
    weight_grads = (jnp.stack([grad_up, grad_down], axis=0)[:, None] * factor).astype(jnp.bfloat16)
    return (outs_up[None], weight_grads, factor * largest)


def solution(mesh):
    placed = (
        P(None, "dp", None),
        P(None, "section", None, "dp", None),
        P(None, "section", "dp", None),
    )
    return jax.shard_map(
        on_device,
        mesh=mesh,
        in_specs=placed,
        out_specs=(P("section", None, "dp", None), P(None, "section", "dp", None), P()),
        check_vma=False,
    )
```

profile of v0, /device:TPU:1, one launch (start us, length us, event | category | flops | bytes accessed | tf_op | source)
XLA Modules:
  0.0 2270.7 jit_solution(9736642941108245857)
XLA Ops:
  7.2 8.8 slice_bitcast_fusion
  20.4 5.9 reshape.126
  26.4 6.0 all-to-all-start.2
  70.9 1005.2 %while.34 = (s32[]{:T(128)}, bf16[16,6144]{1,0:T(8,128)(2,1)S(1)}, bf16[4,16,6144]{2,1,0:T(8,128)(2,1)}, bf16[4,128,6144]{2,1,0:T(8,128)(2,1)}, s32[]{:T(128)}, ...) while((s32[]{:T(128)}, bf16[16,6144]{1,0:T(8,128)(2,1)S(1)}, ...), condition=%wide.region_3.4_spmd, body=%wide.region_0.3_spmd.sunk | while | flops 607322112 | bytes 30082040 | solution.py:71
  73.8 26.5 %all-gather.3.cloned.1.call-done = bf16[128,6144]{1,0:T(8,128)(2,1)} async-done(((bf16[16,6144]{1,0:T(8,128)(2,1)}), bf16[128,6144]{1,0:T(8,128)(2,1)}) %all-gather.3.cloned.1.call-update) | async-done | bytes 1572880 | tf_op jit(solution)/shard_map/while/body/eval_jaxpr/all_gather | solution.py:37
  127.2 26.1 %all-gather.3.cloned.1.call-done = bf16[128,6144]{1,0:T(8,128)(2,1)} async-done(((bf16[16,6144]{1,0:T(8,128)(2,1)}), bf16[128,6144]{1,0:T(8,128)(2,1)}) %all-gather.3.cloned.1.call-update) | async-done | bytes 1572880 | tf_op jit(solution)/shard_map/while/body/eval_jaxpr/all_gather | solution.py:37
  180.2 26.1 %all-gather.3.cloned.1.call-done = bf16[128,6144]{1,0:T(8,128)(2,1)} async-done(((bf16[16,6144]{1,0:T(8,128)(2,1)}), bf16[128,6144]{1,0:T(8,128)(2,1)}) %all-gather.3.cloned.1.call-update) | async-done | bytes 1572880 | tf_op jit(solution)/shard_map/while/body/eval_jaxpr/all_gather | solution.py:37
  233.2 25.8 %all-gather.3.cloned.1.call-done = bf16[128,6144]{1,0:T(8,128)(2,1)} async-done(((bf16[16,6144]{1,0:T(8,128)(2,1)}), bf16[128,6144]{1,0:T(8,128)(2,1)}) %all-gather.3.cloned.1.call-update) | async-done | bytes 1572880 | tf_op jit(solution)/shard_map/while/body/eval_jaxpr/all_gather | solution.py:37
  286.0 25.8 %all-gather.3.cloned.1.call-done = bf16[128,6144]{1,0:T(8,128)(2,1)} async-done(((bf16[16,6144]{1,0:T(8,128)(2,1)}), bf16[128,6144]{1,0:T(8,128)(2,1)}) %all-gather.3.cloned.1.call-update) | async-done | bytes 1572880 | tf_op jit(solution)/shard_map/while/body/eval_jaxpr/all_gather | solution.py:37
  338.7 25.8 %all-gather.3.cloned.1.call-done = bf16[128,6144]{1,0:T(8,128)(2,1)} async-done(((bf16[16,6144]{1,0:T(8,128)(2,1)}), bf16[128,6144]{1,0:T(8,128)(2,1)}) %all-gather.3.cloned.1.call-update) | async-done | bytes 1572880 | tf_op jit(solution)/shard_map/while/body/eval_jaxpr/all_gather | solution.py:37
  391.4 26.1 %all-gather.3.cloned.1.call-done = bf16[128,6144]{1,0:T(8,128)(2,1)} async-done(((bf16[16,6144]{1,0:T(8,128)(2,1)}), bf16[128,6144]{1,0:T(8,128)(2,1)}) %all-gather.3.cloned.1.call-update) | async-done | bytes 1572880 | tf_op jit(solution)/shard_map/while/body/eval_jaxpr/all_gather | solution.py:37
  444.5 26.1 %all-gather.3.cloned.1.call-done = bf16[128,6144]{1,0:T(8,128)(2,1)} async-done(((bf16[16,6144]{1,0:T(8,128)(2,1)}), bf16[128,6144]{1,0:T(8,128)(2,1)}) %all-gather.3.cloned.1.call-update) | async-done | bytes 1572880 | tf_op jit(solution)/shard_map/while/body/eval_jaxpr/all_gather | solution.py:37
  497.5 26.1 %all-gather.3.cloned.1.call-done = bf16[128,6144]{1,0:T(8,128)(2,1)} async-done(((bf16[16,6144]{1,0:T(8,128)(2,1)}), bf16[128,6144]{1,0:T(8,128)(2,1)}) %all-gather.3.cloned.1.call-update) | async-done | bytes 1572880 | tf_op jit(solution)/shard_map/while/body/eval_jaxpr/all_gather | solution.py:37
  550.5 25.8 %all-gather.3.cloned.1.call-done = bf16[128,6144]{1,0:T(8,128)(2,1)} async-done(((bf16[16,6144]{1,0:T(8,128)(2,1)}), bf16[128,6144]{1,0:T(8,128)(2,1)}) %all-gather.3.cloned.1.call-update) | async-done | bytes 1572880 | tf_op jit(solution)/shard_map/while/body/eval_jaxpr/all_gather | solution.py:37
  603.2 26.1 %all-gather.3.cloned.1.call-done = bf16[128,6144]{1,0:T(8,128)(2,1)} async-done(((bf16[16,6144]{1,0:T(8,128)(2,1)}), bf16[128,6144]{1,0:T(8,128)(2,1)}) %all-gather.3.cloned.1.call-update) | async-done | bytes 1572880 | tf_op jit(solution)/shard_map/while/body/eval_jaxpr/all_gather | solution.py:37
  656.3 25.8 %all-gather.3.cloned.1.call-done = bf16[128,6144]{1,0:T(8,128)(2,1)} async-done(((bf16[16,6144]{1,0:T(8,128)(2,1)}), bf16[128,6144]{1,0:T(8,128)(2,1)}) %all-gather.3.cloned.1.call-update) | async-done | bytes 1572880 | tf_op jit(solution)/shard_map/while/body/eval_jaxpr/all_gather | solution.py:37
  709.0 26.1 %all-gather.3.cloned.1.call-done = bf16[128,6144]{1,0:T(8,128)(2,1)} async-done(((bf16[16,6144]{1,0:T(8,128)(2,1)}), bf16[128,6144]{1,0:T(8,128)(2,1)}) %all-gather.3.cloned.1.call-update) | async-done | bytes 1572880 | tf_op jit(solution)/shard_map/while/body/eval_jaxpr/all_gather | solution.py:37
  762.0 25.8 %all-gather.3.cloned.1.call-done = bf16[128,6144]{1,0:T(8,128)(2,1)} async-done(((bf16[16,6144]{1,0:T(8,128)(2,1)}), bf16[128,6144]{1,0:T(8,128)(2,1)}) %all-gather.3.cloned.1.call-update) | async-done | bytes 1572880 | tf_op jit(solution)/shard_map/while/body/eval_jaxpr/all_gather | solution.py:37
  814.7 25.8 %all-gather.3.cloned.1.call-done = bf16[128,6144]{1,0:T(8,128)(2,1)} async-done(((bf16[16,6144]{1,0:T(8,128)(2,1)}), bf16[128,6144]{1,0:T(8,128)(2,1)}) %all-gather.3.cloned.1.call-update) | async-done | bytes 1572880 | tf_op jit(solution)/shard_map/while/body/eval_jaxpr/all_gather | solution.py:37
  867.5 25.8 %all-gather.3.cloned.1.call-done = bf16[128,6144]{1,0:T(8,128)(2,1)} async-done(((bf16[16,6144]{1,0:T(8,128)(2,1)}), bf16[128,6144]{1,0:T(8,128)(2,1)}) %all-gather.3.cloned.1.call-update) | async-done | bytes 1572880 | tf_op jit(solution)/shard_map/while/body/eval_jaxpr/all_gather | solution.py:37
  920.3 25.8 %all-gather.3.cloned.1.call-done = bf16[128,6144]{1,0:T(8,128)(2,1)} async-done(((bf16[16,6144]{1,0:T(8,128)(2,1)}), bf16[128,6144]{1,0:T(8,128)(2,1)}) %all-gather.3.cloned.1.call-update) | async-done | bytes 1572880 | tf_op jit(solution)/shard_map/while/body/eval_jaxpr/all_gather | solution.py:37
  973.0 25.8 %all-gather.3.cloned.1.call-done = bf16[128,6144]{1,0:T(8,128)(2,1)} async-done(((bf16[16,6144]{1,0:T(8,128)(2,1)}), bf16[128,6144]{1,0:T(8,128)(2,1)}) %all-gather.3.cloned.1.call-update) | async-done | bytes 1572880 | tf_op jit(solution)/shard_map/while/body/eval_jaxpr/all_gather | solution.py:37
  1025.8 26.1 %all-gather.3.cloned.1.call-done = bf16[128,6144]{1,0:T(8,128)(2,1)} async-done(((bf16[16,6144]{1,0:T(8,128)(2,1)}), bf16[128,6144]{1,0:T(8,128)(2,1)}) %all-gather.3.cloned.1.call-update) | async-done | bytes 1572880 | tf_op jit(solution)/shard_map/while/body/eval_jaxpr/all_gather | solution.py:37
  1080.5 1020.1 %while.35 = (s32[]{:T(128)}, bf16[16,6144]{1,0:T(8,128)(2,1)S(1)}, bf16[4,16,6144]{2,1,0:T(8,128)(2,1)}, bf16[4,128,6144]{2,1,0:T(8,128)(2,1)}, s32[]{:T(128)}, ...) while((s32[]{:T(128)}, bf16[16,6144]{1,0:T(8,128)(2,1)S(1)}, ...), condition=%wide.region_7.8_spmd, body=%wide.region_4.7_spmd.sunk | while | flops 607322112 | bytes 30082040 | solution.py:71
  1082.4 26.7 %all-gather.5.cloned.1.call-done = bf16[128,6144]{1,0:T(8,128)(2,1)} async-done(((bf16[16,6144]{1,0:T(8,128)(2,1)}), bf16[128,6144]{1,0:T(8,128)(2,1)}) %all-gather.5.cloned.1.call-update) | async-done | bytes 1572880 | tf_op jit(solution)/shard_map/while/body/eval_jaxpr/all_gather | solution.py:37
  1135.1 27.9 %all-gather.5.cloned.1.call-done = bf16[128,6144]{1,0:T(8,128)(2,1)} async-done(((bf16[16,6144]{1,0:T(8,128)(2,1)}), bf16[128,6144]{1,0:T(8,128)(2,1)}) %all-gather.5.cloned.1.call-update) | async-done | bytes 1572880 | tf_op jit(solution)/shard_map/while/body/eval_jaxpr/all_gather | solution.py:37
  1189.0 27.9 %all-gather.5.cloned.1.call-done = bf16[128,6144]{1,0:T(8,128)(2,1)} async-done(((bf16[16,6144]{1,0:T(8,128)(2,1)}), bf16[128,6144]{1,0:T(8,128)(2,1)}) %all-gather.5.cloned.1.call-update) | async-done | bytes 1572880 | tf_op jit(solution)/shard_map/while/body/eval_jaxpr/all_gather | solution.py:37
  1242.8 27.9 %all-gather.5.cloned.1.call-done = bf16[128,6144]{1,0:T(8,128)(2,1)} async-done(((bf16[16,6144]{1,0:T(8,128)(2,1)}), bf16[128,6144]{1,0:T(8,128)(2,1)}) %all-gather.5.cloned.1.call-update) | async-done | bytes 1572880 | tf_op jit(solution)/shard_map/while/body/eval_jaxpr/all_gather | solution.py:37
  1296.7 27.6 %all-gather.5.cloned.1.call-done = bf16[128,6144]{1,0:T(8,128)(2,1)} async-done(((bf16[16,6144]{1,0:T(8,128)(2,1)}), bf16[128,6144]{1,0:T(8,128)(2,1)}) %all-gather.5.cloned.1.call-update) | async-done | bytes 1572880 | tf_op jit(solution)/shard_map/while/body/eval_jaxpr/all_gather | solution.py:37
  1350.2 27.9 %all-gather.5.cloned.1.call-done = bf16[128,6144]{1,0:T(8,128)(2,1)} async-done(((bf16[16,6144]{1,0:T(8,128)(2,1)}), bf16[128,6144]{1,0:T(8,128)(2,1)}) %all-gather.5.cloned.1.call-update) | async-done | bytes 1572880 | tf_op jit(solution)/shard_map/while/body/eval_jaxpr/all_gather | solution.py:37
  1404.1 27.6 %all-gather.5.cloned.1.call-done = bf16[128,6144]{1,0:T(8,128)(2,1)} async-done(((bf16[16,6144]{1,0:T(8,128)(2,1)}), bf16[128,6144]{1,0:T(8,128)(2,1)}) %all-gather.5.cloned.1.call-update) | async-done | bytes 1572880 | tf_op jit(solution)/shard_map/while/body/eval_jaxpr/all_gather | solution.py:37
  1457.6 27.6 %all-gather.5.cloned.1.call-done = bf16[128,6144]{1,0:T(8,128)(2,1)} async-done(((bf16[16,6144]{1,0:T(8,128)(2,1)}), bf16[128,6144]{1,0:T(8,128)(2,1)}) %all-gather.5.cloned.1.call-update) | async-done | bytes 1572880 | tf_op jit(solution)/shard_map/while/body/eval_jaxpr/all_gather | solution.py:37
  1511.2 27.9 %all-gather.5.cloned.1.call-done = bf16[128,6144]{1,0:T(8,128)(2,1)} async-done(((bf16[16,6144]{1,0:T(8,128)(2,1)}), bf16[128,6144]{1,0:T(8,128)(2,1)}) %all-gather.5.cloned.1.call-update) | async-done | bytes 1572880 | tf_op jit(solution)/shard_map/while/body/eval_jaxpr/all_gather | solution.py:37
  1565.1 27.9 %all-gather.5.cloned.1.call-done = bf16[128,6144]{1,0:T(8,128)(2,1)} async-done(((bf16[16,6144]{1,0:T(8,128)(2,1)}), bf16[128,6144]{1,0:T(8,128)(2,1)}) %all-gather.5.cloned.1.call-update) | async-done | bytes 1572880 | tf_op jit(solution)/shard_map/while/body/eval_jaxpr/all_gather | solution.py:37
  1618.9 27.6 %all-gather.5.cloned.1.call-done = bf16[128,6144]{1,0:T(8,128)(2,1)} async-done(((bf16[16,6144]{1,0:T(8,128)(2,1)}), bf16[128,6144]{1,0:T(8,128)(2,1)}) %all-gather.5.cloned.1.call-update) | async-done | bytes 1572880 | tf_op jit(solution)/shard_map/while/body/eval_jaxpr/all_gather | solution.py:37
  1672.5 27.9 %all-gather.5.cloned.1.call-done = bf16[128,6144]{1,0:T(8,128)(2,1)} async-done(((bf16[16,6144]{1,0:T(8,128)(2,1)}), bf16[128,6144]{1,0:T(8,128)(2,1)}) %all-gather.5.cloned.1.call-update) | async-done | bytes 1572880 | tf_op jit(solution)/shard_map/while/body/eval_jaxpr/all_gather | solution.py:37
  1726.3 27.9 %all-gather.5.cloned.1.call-done = bf16[128,6144]{1,0:T(8,128)(2,1)} async-done(((bf16[16,6144]{1,0:T(8,128)(2,1)}), bf16[128,6144]{1,0:T(8,128)(2,1)}) %all-gather.5.cloned.1.call-update) | async-done | bytes 1572880 | tf_op jit(solution)/shard_map/while/body/eval_jaxpr/all_gather | solution.py:37
  1780.2 27.6 %all-gather.5.cloned.1.call-done = bf16[128,6144]{1,0:T(8,128)(2,1)} async-done(((bf16[16,6144]{1,0:T(8,128)(2,1)}), bf16[128,6144]{1,0:T(8,128)(2,1)}) %all-gather.5.cloned.1.call-update) | async-done | bytes 1572880 | tf_op jit(solution)/shard_map/while/body/eval_jaxpr/all_gather | solution.py:37
  1833.7 27.9 %all-gather.5.cloned.1.call-done = bf16[128,6144]{1,0:T(8,128)(2,1)} async-done(((bf16[16,6144]{1,0:T(8,128)(2,1)}), bf16[128,6144]{1,0:T(8,128)(2,1)}) %all-gather.5.cloned.1.call-update) | async-done | bytes 1572880 | tf_op jit(solution)/shard_map/while/body/eval_jaxpr/all_gather | solution.py:37
  1887.6 27.9 %all-gather.5.cloned.1.call-done = bf16[128,6144]{1,0:T(8,128)(2,1)} async-done(((bf16[16,6144]{1,0:T(8,128)(2,1)}), bf16[128,6144]{1,0:T(8,128)(2,1)}) %all-gather.5.cloned.1.call-update) | async-done | bytes 1572880 | tf_op jit(solution)/shard_map/while/body/eval_jaxpr/all_gather | solution.py:37
  1941.4 27.6 %all-gather.5.cloned.1.call-done = bf16[128,6144]{1,0:T(8,128)(2,1)} async-done(((bf16[16,6144]{1,0:T(8,128)(2,1)}), bf16[128,6144]{1,0:T(8,128)(2,1)}) %all-gather.5.cloned.1.call-update) | async-done | bytes 1572880 | tf_op jit(solution)/shard_map/while/body/eval_jaxpr/all_gather | solution.py:37
  1995.0 27.6 %all-gather.5.cloned.1.call-done = bf16[128,6144]{1,0:T(8,128)(2,1)} async-done(((bf16[16,6144]{1,0:T(8,128)(2,1)}), bf16[128,6144]{1,0:T(8,128)(2,1)}) %all-gather.5.cloned.1.call-update) | async-done | bytes 1572880 | tf_op jit(solution)/shard_map/while/body/eval_jaxpr/all_gather | solution.py:37
  2048.5 27.9 %all-gather.5.cloned.1.call-done = bf16[128,6144]{1,0:T(8,128)(2,1)} async-done(((bf16[16,6144]{1,0:T(8,128)(2,1)}), bf16[128,6144]{1,0:T(8,128)(2,1)}) %all-gather.5.cloned.1.call-update) | async-done | bytes 1572880 | tf_op jit(solution)/shard_map/while/body/eval_jaxpr/all_gather | solution.py:37
  2100.5 10.1 abs_reduce_fusion.1
  2110.7 6.4 abs_reduce_fusion
  2118.3 66.8 %psum.7 = f32[]{:T(128)} all-reduce(f32[]{:T(128)S(6)} %add.130), channel_id=1, replica_groups=mesh['section'=16,'dp'=8] {'section','dp'}, use_global_device_ids=true, to_apply=%region_12.13 | all-reduce | flops 1 | bytes 8 | tf_op jit(solution)/shard_map/psum | solution.py:116
  2187.1 63.8 %pmax.7 = f32[]{:T(128)} all-reduce(f32[]{:T(128)S(6)} %max.20), channel_id=1, replica_groups=mesh['section'=16,'dp'=8] {'section','dp'}, use_global_device_ids=true, to_apply=%region_15.16 | all-reduce | flops 1 | bytes 8 | tf_op jit(solution)/shard_map/pmax | solution.py:117
  2251.5 11.5 fusion.18
  (864 shorter events, 1050.6 us)
Async XLA Ops:
  26.4 17.4 all-to-all-start.2
  43.7 14.3 all-to-all-start.3
  70.9 29.4 %all-gather.3.cloned.1.call-start = ((), (), s32[]{:S(2)}) async-start(), calls=%async_computation.4 | async-start | bytes 1769472 | tf_op jit(solution)/shard_map/while/body/eval_jaxpr/all_gather | solution.py:37
  124.4 28.9 %all-gather.3.cloned.1.call-start = ((), (), s32[]{:S(2)}) async-start(), calls=%async_computation.4 | async-start | bytes 1769472 | tf_op jit(solution)/shard_map/while/body/eval_jaxpr/all_gather | solution.py:37
  158.4 9.5 all-to-all-start
  177.4 28.9 %all-gather.3.cloned.1.call-start = ((), (), s32[]{:S(2)}) async-start(), calls=%async_computation.4 | async-start | bytes 1769472 | tf_op jit(solution)/shard_map/while/body/eval_jaxpr/all_gather | solution.py:37
  230.5 28.6 %all-gather.3.cloned.1.call-start = ((), (), s32[]{:S(2)}) async-start(), calls=%async_computation.4 | async-start | bytes 1769472 | tf_op jit(solution)/shard_map/while/body/eval_jaxpr/all_gather | solution.py:37
  283.2 28.6 %all-gather.3.cloned.1.call-start = ((), (), s32[]{:S(2)}) async-start(), calls=%async_computation.4 | async-start | bytes 1769472 | tf_op jit(solution)/shard_map/while/body/eval_jaxpr/all_gather | solution.py:37
  316.9 9.5 all-to-all-start
  335.9 28.6 %all-gather.3.cloned.1.call-start = ((), (), s32[]{:S(2)}) async-start(), calls=%async_computation.4 | async-start | bytes 1769472 | tf_op jit(solution)/shard_map/while/body/eval_jaxpr/all_gather | solution.py:37
  388.6 28.9 %all-gather.3.cloned.1.call-start = ((), (), s32[]{:S(2)}) async-start(), calls=%async_computation.4 | async-start | bytes 1769472 | tf_op jit(solution)/shard_map/while/body/eval_jaxpr/all_gather | solution.py:37
  422.7 9.5 all-to-all-start
  441.7 28.9 %all-gather.3.cloned.1.call-start = ((), (), s32[]{:S(2)}) async-start(), calls=%async_computation.4 | async-start | bytes 1769472 | tf_op jit(solution)/shard_map/while/body/eval_jaxpr/all_gather | solution.py:37
  475.7 9.5 all-to-all-start
  494.7 28.9 %all-gather.3.cloned.1.call-start = ((), (), s32[]{:S(2)}) async-start(), calls=%async_computation.4 | async-start | bytes 1769472 | tf_op jit(solution)/shard_map/while/body/eval_jaxpr/all_gather | solution.py:37
  547.7 28.6 %all-gather.3.cloned.1.call-start = ((), (), s32[]{:S(2)}) async-start(), calls=%async_computation.4 | async-start | bytes 1769472 | tf_op jit(solution)/shard_map/while/body/eval_jaxpr/all_gather | solution.py:37
  581.4 9.5 all-to-all-start
  600.5 28.9 %all-gather.3.cloned.1.call-start = ((), (), s32[]{:S(2)}) async-start(), calls=%async_computation.4 | async-start | bytes 1769472 | tf_op jit(solution)/shard_map/while/body/eval_jaxpr/all_gather | solution.py:37
  653.5 28.6 %all-gather.3.cloned.1.call-start = ((), (), s32[]{:S(2)}) async-start(), calls=%async_computation.4 | async-start | bytes 1769472 | tf_op jit(solution)/shard_map/while/body/eval_jaxpr/all_gather | solution.py:37
  706.2 28.9 %all-gather.3.cloned.1.call-start = ((), (), s32[]{:S(2)}) async-start(), calls=%async_computation.4 | async-start | bytes 1769472 | tf_op jit(solution)/shard_map/while/body/eval_jaxpr/all_gather | solution.py:37
  759.2 28.6 %all-gather.3.cloned.1.call-start = ((), (), s32[]{:S(2)}) async-start(), calls=%async_computation.4 | async-start | bytes 1769472 | tf_op jit(solution)/shard_map/while/body/eval_jaxpr/all_gather | solution.py:37
  812.0 28.6 %all-gather.3.cloned.1.call-start = ((), (), s32[]{:S(2)}) async-start(), calls=%async_computation.4 | async-start | bytes 1769472 | tf_op jit(solution)/shard_map/while/body/eval_jaxpr/all_gather | solution.py:37
  864.7 28.6 %all-gather.3.cloned.1.call-start = ((), (), s32[]{:S(2)}) async-start(), calls=%async_computation.4 | async-start | bytes 1769472 | tf_op jit(solution)/shard_map/while/body/eval_jaxpr/all_gather | solution.py:37
  917.5 28.6 %all-gather.3.cloned.1.call-start = ((), (), s32[]{:S(2)}) async-start(), calls=%async_computation.4 | async-start | bytes 1769472 | tf_op jit(solution)/shard_map/while/body/eval_jaxpr/all_gather | solution.py:37
  970.2 28.6 %all-gather.3.cloned.1.call-start = ((), (), s32[]{:S(2)}) async-start(), calls=%async_computation.4 | async-start | bytes 1769472 | tf_op jit(solution)/shard_map/while/body/eval_jaxpr/all_gather | solution.py:37
  1023.0 28.9 %all-gather.3.cloned.1.call-start = ((), (), s32[]{:S(2)}) async-start(), calls=%async_computation.4 | async-start | bytes 1769472 | tf_op jit(solution)/shard_map/while/body/eval_jaxpr/all_gather | solution.py:37
  1080.5 28.6 %all-gather.5.cloned.1.call-start = ((), (), s32[]{:S(2)}) async-start(), calls=%async_computation.5 | async-start | bytes 1769472 | tf_op jit(solution)/shard_map/while/body/eval_jaxpr/all_gather | solution.py:37
  1133.2 29.7 %all-gather.5.cloned.1.call-start = ((), (), s32[]{:S(2)}) async-start(), calls=%async_computation.5 | async-start | bytes 1769472 | tf_op jit(solution)/shard_map/while/body/eval_jaxpr/all_gather | solution.py:37
  1168.1 9.5 all-to-all-start.1
  1187.1 29.7 %all-gather.5.cloned.1.call-start = ((), (), s32[]{:S(2)}) async-start(), calls=%async_computation.5 | async-start | bytes 1769472 | tf_op jit(solution)/shard_map/while/body/eval_jaxpr/all_gather | solution.py:37
  1241.0 29.7 %all-gather.5.cloned.1.call-start = ((), (), s32[]{:S(2)}) async-start(), calls=%async_computation.5 | async-start | bytes 1769472 | tf_op jit(solution)/shard_map/while/body/eval_jaxpr/all_gather | solution.py:37
  1294.8 29.4 %all-gather.5.cloned.1.call-start = ((), (), s32[]{:S(2)}) async-start(), calls=%async_computation.5 | async-start | bytes 1769472 | tf_op jit(solution)/shard_map/while/body/eval_jaxpr/all_gather | solution.py:37
  1348.4 29.7 %all-gather.5.cloned.1.call-start = ((), (), s32[]{:S(2)}) async-start(), calls=%async_computation.5 | async-start | bytes 1769472 | tf_op jit(solution)/shard_map/while/body/eval_jaxpr/all_gather | solution.py:37
  1402.2 29.4 %all-gather.5.cloned.1.call-start = ((), (), s32[]{:S(2)}) async-start(), calls=%async_computation.5 | async-start | bytes 1769472 | tf_op jit(solution)/shard_map/while/body/eval_jaxpr/all_gather | solution.py:37
  1455.8 29.4 %all-gather.5.cloned.1.call-start = ((), (), s32[]{:S(2)}) async-start(), calls=%async_computation.5 | async-start | bytes 1769472 | tf_op jit(solution)/shard_map/while/body/eval_jaxpr/all_gather | solution.py:37
  1509.3 29.7 %all-gather.5.cloned.1.call-start = ((), (), s32[]{:S(2)}) async-start(), calls=%async_computation.5 | async-start | bytes 1769472 | tf_op jit(solution)/shard_map/while/body/eval_jaxpr/all_gather | solution.py:37
  1563.2 29.7 %all-gather.5.cloned.1.call-start = ((), (), s32[]{:S(2)}) async-start(), calls=%async_computation.5 | async-start | bytes 1769472 | tf_op jit(solution)/shard_map/while/body/eval_jaxpr/all_gather | solution.py:37
  1617.1 29.4 %all-gather.5.cloned.1.call-start = ((), (), s32[]{:S(2)}) async-start(), calls=%async_computation.5 | async-start | bytes 1769472 | tf_op jit(solution)/shard_map/while/body/eval_jaxpr/all_gather | solution.py:37
  1670.6 29.7 %all-gather.5.cloned.1.call-start = ((), (), s32[]{:S(2)}) async-start(), calls=%async_computation.5 | async-start | bytes 1769472 | tf_op jit(solution)/shard_map/while/body/eval_jaxpr/all_gather | solution.py:37
  1724.5 29.7 %all-gather.5.cloned.1.call-start = ((), (), s32[]{:S(2)}) async-start(), calls=%async_computation.5 | async-start | bytes 1769472 | tf_op jit(solution)/shard_map/while/body/eval_jaxpr/all_gather | solution.py:37
  1778.3 29.4 %all-gather.5.cloned.1.call-start = ((), (), s32[]{:S(2)}) async-start(), calls=%async_computation.5 | async-start | bytes 1769472 | tf_op jit(solution)/shard_map/while/body/eval_jaxpr/all_gather | solution.py:37
  1831.9 29.7 %all-gather.5.cloned.1.call-start = ((), (), s32[]{:S(2)}) async-start(), calls=%async_computation.5 | async-start | bytes 1769472 | tf_op jit(solution)/shard_map/while/body/eval_jaxpr/all_gather | solution.py:37
  1885.7 29.7 %all-gather.5.cloned.1.call-start = ((), (), s32[]{:S(2)}) async-start(), calls=%async_computation.5 | async-start | bytes 1769472 | tf_op jit(solution)/shard_map/while/body/eval_jaxpr/all_gather | solution.py:37
  1920.6 9.5 all-to-all-start.1
  1939.6 29.4 %all-gather.5.cloned.1.call-start = ((), (), s32[]{:S(2)}) async-start(), calls=%async_computation.5 | async-start | bytes 1769472 | tf_op jit(solution)/shard_map/while/body/eval_jaxpr/all_gather | solution.py:37
  1993.1 29.4 %all-gather.5.cloned.1.call-start = ((), (), s32[]{:S(2)}) async-start(), calls=%async_computation.5 | async-start | bytes 1769472 | tf_op jit(solution)/shard_map/while/body/eval_jaxpr/all_gather | solution.py:37
  2046.7 29.7 %all-gather.5.cloned.1.call-start = ((), (), s32[]{:S(2)}) async-start(), calls=%async_computation.5 | async-start | bytes 1769472 | tf_op jit(solution)/shard_map/while/body/eval_jaxpr/all_gather | solution.py:37
  2081.5 9.5 all-to-all-start.1
  (147 other events, 1899.4 us)
Sparse Core Ops, SparseCore 0:
  73.4 26.7 all-gather.2
  126.9 26.3 all-gather.2
  179.9 26.3 all-gather.2
  232.7 26.3 all-gather.2
  285.4 26.3 all-gather.2
  338.1 26.3 all-gather.2
  391.2 26.3 all-gather.2
  444.2 26.3 all-gather.2
  497.2 26.3 all-gather.2
  549.9 26.3 all-gather.2
  603.0 26.3 all-gather.2
  655.7 26.3 all-gather.2
  708.7 26.3 all-gather.2
  761.4 26.3 all-gather.2
  814.2 26.3 all-gather.2
  866.9 26.3 all-gather.2
  919.7 26.3 all-gather.2
  972.4 26.3 all-gather.2
  1025.5 26.3 all-gather.2
  1082.7 26.3 all-gather.4
  1135.8 27.1 all-gather.4
  1189.6 27.1 all-gather.4
  1243.5 27.1 all-gather.4
  1297.0 27.1 all-gather.4
  1350.9 27.1 all-gather.4
  1404.4 27.1 all-gather.4
  1458.0 27.1 all-gather.4
  1511.8 27.1 all-gather.4
  1565.7 27.1 all-gather.4
  1619.3 27.1 all-gather.4
  1673.1 27.1 all-gather.4
  1727.0 27.1 all-gather.4
  1780.5 27.1 all-gather.4
  1834.4 27.1 all-gather.4
  1888.2 27.1 all-gather.4
  1941.8 27.1 all-gather.4
  1995.3 27.1 all-gather.4
  2049.2 27.1 all-gather.4
where the time goes:
time: 2280 us; the launch traced here: 2270 us
  waiting for transfers between devices  1290 us (57%)
  other arithmetic  335 us (15%)
  starting transfers between devices  229 us (10%)
  matrix products  211 us (9%)
  blocking collectives  131 us (6%)
  local copies, waits for them, and re-layouts  56.3 us (2%)
    all_gather x38, waiting for transfers between devices, backward_pass(): gathered = lax.all_gather(cot_in, 'dp', axis=0, tiled=True)  1020 us
    all_to_all x38, waiting for transfers between devices, backward_pass(): lax.all_to_all(partial_grad, 'dp', split_axis=0, concat_axis=1, tiled=True)  203 us
    dot_general x38, matrix products, backward_pass(): lax.dot_general(gathered, rows, (((1,), (1,)), ((), ())), preferred_eleme...  195 us
    all_to_all x38, starting transfers between devices, backward_pass(): lax.all_to_all(partial_grad, 'dp', split_axis=0, concat_axis=1, tiled=True)  135 us
    select_n x38, other arithmetic, advance(): stashed = jnp.where(active_now, updated_stashed, stashed)  111 us
    ppermute x38, starting transfers between devices, passed_along(): return lax.ppermute(value, axis, pairs)  83.5 us
    select_n x38, other arithmetic, advance(): outputs = jnp.where(active_now, updated_outputs, outputs)  71 us
    psum x1, blocking collectives, on_device(): total = lax.psum(local_sum, ('section', 'dp'))  66.8 us
  transfers between devices with their start and end apart: 116, of which 114 were waited for; matrix products, arithmetic and copies ran while one was open for 8% of the time, Pallas kernels for 0%

commit v1 on v0

v1 whole, which is shorter than its diff:
```python
import functools

import jax
import jax.numpy as jnp
from jax import lax
from jax.experimental import pallas as pl
from jax.experimental.pallas import tpu as pltpu
from jax.sharding import PartitionSpec as P

epsilon = 1e-05
MESH = pl.DeviceIdType.MESH
T = 32
LAG = (3, 5)


def relay_kernel(
    ns, nb, hs, nc, wt_hbm, xp_hbm, cot_hbm, coef, h_t, x_own,
    grads, leaving, stats,
    wt, xg, u, q, sbuf, obuf, gtile, stat_dp, stat_sec, stat_me,
    recv, relay_sem, send_sem, own_send, own_recv, load_sem, tile_sem, stat_send, stat_recv,
):
    f32 = jnp.float32
    s = lax.axis_index("section")
    me = lax.axis_index("dp")
    y = lax.div(me, 2)
    c = lax.rem(me, 2)
    ny = nb // 2
    partner = me + 1 - 2 * c
    per_owner = nc // nb
    wide = 2 * hs + 128

    loads = []
    for leg in range(2):
        loads.append(pltpu.make_async_copy(wt_hbm.at[leg], wt.at[leg], load_sem.at[leg, 0]))
        loads.append(pltpu.make_async_copy(xp_hbm.at[leg], xg.at[leg], load_sem.at[leg, 1]))
    for copy in loads:
        copy.start()

    barrier = pltpu.get_barrier_semaphore()

    def greet(section, dp):
        pl.semaphore_signal(
            barrier, inc=1, device_id={"section": section, "dp": dp}, device_id_type=MESH
        )

    for j in range(1, nb):
        greet(s, lax.rem(me + j, nb))
    for j in range(1, ns):
        greet(lax.rem(s + j, ns), me)

    @pl.when(s < ns - 1)
    def _():
        for j in range(ny):
            greet(s + 1, 2 * j + c)

    @pl.when(s > 0)
    def _():
        for j in range(ny):
            greet(s - 1, 2 * j + c)

    pl.semaphore_wait(
        barrier, nb - 1 + ns - 1 + ny * jnp.where(s < ns - 1, 1, 0) + ny * jnp.where(s > 0, 1, 0)
    )

    @pl.when(s == 0)
    def _():
        copy = pltpu.make_async_copy(cot_hbm, u.at[0], load_sem.at[0, 2])
        copy.start()
        copy.wait()

    for copy in loads:
        copy.wait()

    for leg in range(2):
        def fill(k, _, leg=leg):
            total = jnp.zeros((T, hs), f32)
            for b in range(nb):
                total += jnp.dot(xg[leg, k, b], wt[leg, b], preferred_element_type=f32)
            q[leg, k] = total
            return 0

        lax.fori_loop(0, nc, fill, 0)

    def step(leg, k):
        first = (s == 0) if leg == 0 else False
        acc = jnp.zeros((T, hs), f32)

        def arrived(b):
            block = u.at[leg, k, b]
            pltpu.make_async_copy(block, block, recv.at[leg, k, b]).wait()

        for dy in (0, 1, 3, 2):
            b = 2 * lax.rem(y + dy, ny) + c

            def pass_on(b=b):
                arrived(b)
                pltpu.make_async_remote_copy(
                    src_ref=u.at[leg, k, b],
                    dst_ref=u.at[leg, k, b],
                    send_sem=relay_sem.at[leg, k],
                    recv_sem=recv.at[leg, k, b],
                    device_id={"section": s, "dp": partner},
                    device_id_type=MESH,
                ).start()

            if leg == 0:
                pl.when(s > 0)(pass_on)
            else:
                pass_on()
            acc += jnp.dot(u[leg, k, b][:, : 2 * hs], wt[leg, b], preferred_element_type=f32)
        for dy in (0, 1, 3, 2):
            b = 2 * lax.rem(y + dy, ny) + 1 - c
            if leg == 0:
                pl.when(s > 0)(functools.partial(arrived, b))
            else:
                arrived(b)
            acc += jnp.dot(u[leg, k, b][:, : 2 * hs], wt[leg, b], preferred_element_type=f32)
        kap = u[leg, k, 0][:, 2 * hs :].astype(f32)
        for b in range(1, nb):
            kap += u[leg, k, b][:, 2 * hs :].astype(f32)
        kap = jnp.concatenate([kap] * (hs // 128), axis=1)
        dh = acc - kap * q[leg, k]
        mine = u[leg, k, me].astype(f32)
        x_mine = xg[leg, k, me].astype(f32)
        new_a = mine[:, :hs] - kap * x_mine[:, :hs] + coef[leg, 0, k] * dh
        new_g = mine[:, hs : 2 * hs] - kap * x_mine[:, hs:] + coef[leg, 1, k] * dh
        part = jnp.sum(coef[leg, 2, k] * dh, axis=1, keepdims=True)
        sbuf[leg, k, :, :hs] = new_a.astype(jnp.bfloat16)
        sbuf[leg, k, :, hs : 2 * hs] = new_g.astype(jnp.bfloat16)
        sbuf[leg, k, :, 2 * hs :] = jnp.broadcast_to(part, (T, 128)).astype(jnp.bfloat16)

        def send(section, to_leg, dys):
            for dy in dys:
                pltpu.make_async_remote_copy(
                    src_ref=sbuf.at[leg, k],
                    dst_ref=u.at[to_leg, k, me],
                    send_sem=send_sem.at[leg, k],
                    recv_sem=recv.at[to_leg, k, me],
                    device_id={"section": section, "dp": 2 * lax.rem(y + dy, ny) + c},
                    device_id_type=MESH,
                ).start()

        if leg == 0:
            @pl.when(s < ns - 1)
            def _():
                send(s + 1, 0, (2, 1, 3, 0))

            @pl.when(s == ns - 1)
            def _():
                send(s, 1, (2, 1, 3))
                pltpu.make_async_copy(sbuf.at[0, k], u.at[1, k, me], recv.at[1, k, me]).start()
        else:
            @pl.when(s > 0)
            def _():
                send(s - 1, 1, (2, 1, 3, 0))

            owner = lax.div(k, per_owner)
            half = lax.rem(k, per_owner)

            @pl.when(owner == me)
            def _():
                pltpu.make_async_copy(
                    sbuf.at[1, k], obuf.at[half, me], own_recv.at[half, me]
                ).start()

            @pl.when(owner != me)
            def _():
                pltpu.make_async_remote_copy(
                    src_ref=sbuf.at[1, k],
                    dst_ref=obuf.at[half, me],
                    send_sem=own_send.at[k],
                    recv_sem=own_recv.at[half, me],
                    device_id={"section": s, "dp": owner},
                    device_id_type=MESH,
                ).start()

        wide_kap = jnp.concatenate([kap, kap], axis=1)
        for b in range(nb):
            value = u[leg, k, b][:, : 2 * hs].astype(f32) - wide_kap * xg[leg, k, b].astype(f32)
            xg[leg, k, b] = value.astype(jnp.bfloat16)

    lag = jnp.minimum(nc, LAG[0] + LAG[1] * (ns - 1 - s))

    def advance(i, _):
        @pl.when(i < nc)
        def _():
            step(0, i)

        @pl.when(i >= lag)
        def _():
            step(1, i - lag)

        return 0

    lax.fori_loop(0, nc + lag, advance, 0)

    stat_me[...] = jnp.zeros_like(stat_me)
    for leg in range(2):
        def tile(j, _, leg=leg):
            slot = lax.rem(j, 2)
            b = lax.div(j, 2)
            columns = pl.ds(pl.multiple_of(slot * nb * hs + b * hs, 128), hs)
            copy = pltpu.make_async_copy(
                gtile.at[slot], grads.at[1 - leg, 0, :, columns], tile_sem.at[slot]
            )

            @pl.when(j >= 2)
            def _():
                copy.wait()

            offset = pl.multiple_of(slot * hs, 128)
            right = xg[leg, :, b, :, pl.ds(offset, hs)].reshape(nc * T, hs)
            out = jnp.dot(h_t[leg], right, preferred_element_type=f32)
            gtile[slot] = out.astype(jnp.bfloat16)
            copy.start()
            folded = out.reshape(hs // 8, 8, hs)
            squares = jnp.sum(folded * folded, axis=0)
            tops = jnp.max(jnp.abs(folded), axis=0)
            for lane in range(0, hs, 128):
                stat_me[0] += squares[:, lane : lane + 128]
                stat_me[1] = jnp.maximum(stat_me[1], tops[:, lane : lane + 128])
            return 0

        lax.fori_loop(0, 2 * nb, tile, 0)
        for slot in range(2):
            pltpu.make_async_copy(
                gtile.at[slot], grads.at[1 - leg, 0, :, pl.ds(0, hs)], tile_sem.at[slot]
            ).wait()

    stat_dp[me] = stat_me[...]
    for j in range(1, nb):
        pltpu.make_async_remote_copy(
            src_ref=stat_me, dst_ref=stat_dp.at[me], send_sem=stat_send.at[0], recv_sem=stat_recv.at[0],
            device_id={"section": s, "dp": lax.rem(me + j, nb)}, device_id_type=MESH,
        ).start()
    some = stat_dp.at[pl.ds(0, nb - 1)]
    pltpu.make_async_copy(some, some, stat_recv.at[0]).wait()
    pltpu.make_async_copy(some, some, stat_send.at[0]).wait()
    both = stat_dp[...]
    stat_me[0] = jnp.sum(both[:, 0], axis=0)
    stat_me[1] = jnp.max(both[:, 1], axis=0)
    stat_sec[s] = stat_me[...]
    for j in range(1, ns):
        pltpu.make_async_remote_copy(
            src_ref=stat_me, dst_ref=stat_sec.at[s], send_sem=stat_send.at[1], recv_sem=stat_recv.at[1],
            device_id={"section": lax.rem(s + j, ns), "dp": me}, device_id_type=MESH,
        ).start()

    for half in range(per_owner):
        for b in range(nb):
            block = obuf.at[half, b]
            pltpu.make_async_copy(block, block, own_recv.at[half, b]).wait()
        kap = jnp.sum(obuf[half, :, :, 2 * hs :].astype(f32), axis=0)
        kap = jnp.concatenate([kap] * (hs // 128), axis=1)
        rows = pl.ds(half * T, T)
        for b in range(nb):
            for part in range(2):
                columns = pl.ds(part * nb * hs + b * hs, hs)
                value = obuf[half, b, :, part * hs : (part + 1) * hs].astype(f32)
                value -= kap * x_own[rows, columns].astype(f32)
                leaving[rows, columns] = value.astype(jnp.bfloat16)

    some = stat_sec.at[pl.ds(0, ns - 1)]
    pltpu.make_async_copy(some, some, stat_recv.at[1]).wait()
    pltpu.make_async_copy(some, some, stat_send.at[1]).wait()
    both = stat_sec[...]
    stats[0] = jnp.sum(both[:, 0], axis=0)
    stats[1] = jnp.max(both[:, 1], axis=0)

    def drain(k, _):
        four = u.at[0, k, pl.ds(0, ny)]
        three = u.at[0, k, pl.ds(0, ny - 1)]
        one = u.at[0, k, 0]

        @pl.when(s > 0)
        def _():
            pltpu.make_async_copy(four, four, relay_sem.at[0, k]).wait()
            pltpu.make_async_copy(four, four, send_sem.at[1, k]).wait()

        pltpu.make_async_copy(four, four, relay_sem.at[1, k]).wait()

        @pl.when(s < ns - 1)
        def _():
            pltpu.make_async_copy(four, four, send_sem.at[0, k]).wait()

        @pl.when(s == ns - 1)
        def _():
            pltpu.make_async_copy(three, three, send_sem.at[0, k]).wait()

        @pl.when(lax.div(k, per_owner) != me)
        def _():
            pltpu.make_async_copy(one, one, own_send.at[k]).wait()

        return 0

    lax.fori_loop(0, nc, drain, 0)


def passed_along(value, by):
    length = lax.axis_size("section")
    pairs = [(i, i + by) for i in range(length) if 0 <= i + by < length]
    return lax.ppermute(value, "section", pairs)


def on_device(cotangent, saved_inputs, weights):
    f32, bf16 = jnp.float32, jnp.bfloat16
    ns = lax.axis_size("section")
    nb = lax.axis_size("dp")
    s = lax.axis_index("section")
    hs, width = weights.shape[2:]
    rows = saved_inputs.shape[2] * saved_inputs.shape[3]
    per_owner = rows // T
    nc = per_owner * nb
    wide = 2 * hs + 128

    own = saved_inputs[:, 0].reshape(2, rows, width)[::-1]
    from_above = passed_along(own[0], 1)
    from_below = jnp.where(s == ns - 1, own[0], passed_along(own[1], -1))

    def blocked(value):
        legs = value.shape[0]
        value = value.reshape(legs, per_owner, T, 2, nb, hs)
        return value.transpose(0, 1, 4, 2, 3, 5).reshape(legs, per_owner, nb, T, 2 * hs)

    before = lax.all_gather(
        blocked(jnp.stack([from_above, from_below])), "dp", axis=1, tiled=True
    )
    start = blocked(cotangent.reshape(1, rows, width))[0]
    start = jnp.pad(start, ((0, 0), (0, 0), (0, 0), (0, 128)))
    start = lax.all_gather(start, "dp", axis=0, tiled=True)

    scale = lax.rsqrt(jnp.mean(jnp.square(own.astype(f32)), axis=-1) + epsilon)
    scale = lax.all_gather(scale, "dp", axis=1, tiled=True)[..., None]
    mine = lax.all_to_all(
        own.reshape(2, rows, 2, nb, hs), "dp", split_axis=3, concat_axis=1, tiled=True
    )[:, :, :, 0].astype(f32)
    first = mine[:, :, 0] * scale
    gate_in = mine[:, :, 1] * scale
    gated = jax.nn.sigmoid(gate_in)
    feats = first * gated
    coef = jnp.stack(
        [
            scale * gated,
            scale * feats * (1.0 - gated),
            scale * scale * feats * (1.0 + (1.0 - gated) * gate_in) / width,
        ],
        axis=1,
    ).reshape(2, 3, nc, T, hs)
    h_t = feats.astype(bf16).transpose(0, 2, 1)
    wt = weights[::-1, 0].reshape(2, hs, 2, nb, hs).transpose(0, 3, 2, 4, 1)
    wt = wt.reshape(2, nb, 2 * hs, hs)

    vmem = pl.BlockSpec(memory_space=pltpu.VMEM)
    hbm = pl.BlockSpec(memory_space=pl.ANY)
    dma = pltpu.SemaphoreType.DMA
    grads, leaving, stats = pl.pallas_call(
        functools.partial(relay_kernel, ns, nb, hs, nc),
        out_shape=(
            jax.ShapeDtypeStruct((2, 1, hs, width), bf16),
            jax.ShapeDtypeStruct((rows, width), bf16),
            jax.ShapeDtypeStruct((2, 8, 128), f32),
        ),
        in_specs=[hbm, hbm, hbm, vmem, vmem, vmem],
        out_specs=(hbm, vmem, vmem),
        scratch_shapes=[
            pltpu.VMEM((2, nb, 2 * hs, hs), bf16),
            pltpu.VMEM((2, nc, nb, T, 2 * hs), bf16),
            pltpu.VMEM((2, nc, nb, T, wide), bf16),
            pltpu.VMEM((2, nc, T, hs), f32),
            pltpu.VMEM((2, nc, T, wide), bf16),
            pltpu.VMEM((per_owner, nb, T, wide), bf16),
            pltpu.VMEM((2, hs, hs), bf16),
            pltpu.VMEM((nb, 2, 8, 128), f32),
            pltpu.VMEM((ns, 2, 8, 128), f32),
            pltpu.VMEM((2, 8, 128), f32),
            dma((2, nc, nb)),
            dma((2, nc)),
            dma((2, nc)),
            dma((nc,)),
            dma((per_owner, nb)),
            dma((2, 3)),
            dma((2,)),
            dma((2,)),
            dma((2,)),
        ],
        compiler_params=pltpu.CompilerParams(
            collective_id=0, has_side_effects=True, vmem_limit_bytes=58 * 2**20
        ),
        name="relay",
    )(wt, before, start, coef, h_t, own[1])

    total = jnp.sum(stats[0])
    largest = jnp.max(stats[1])
    limit = 0.5 * jnp.sqrt(jnp.float32(2 * ns * (width // 2) * width))
    factor = jnp.minimum(jnp.float32(1.0), limit / jnp.sqrt(total))
    weight_grads = (grads.astype(f32) * factor).astype(bf16)
    return (leaving.reshape(1, *cotangent.shape), weight_grads, factor * largest)


def solution(mesh):
    placed = (
        P(None, "dp", None),
        P(None, "section", None, "dp", None),
        P(None, "section", "dp", None),
    )
    return jax.shard_map(
        on_device,
        mesh=mesh,
        in_specs=placed,
        out_specs=(P("section", None, "dp", None), P(None, "section", "dp", None), P()),
        check_vma=False,
    )
```

time: 2280 us -> 632 us (0.28)
  waiting for transfers between devices: 1290 us -> 32.3 us
  Pallas kernels: 0 us -> 473 us
  other arithmetic: 335 us -> 18.8 us
  starting transfers between devices: 229 us -> 12.5 us
  matrix products: 211 us -> 0 us
  blocking collectives: 131 us -> 26.8 us
    all_gather x38 -> x2, waiting for transfers between devices: 1020 us -> 14.7 us  [the longest x1 14.7 us: on_device(): lax.all_gather(blocked(jnp.stack([from_above, from_below])), 'dp', axis=1...]
    pallas_call x0 -> x1, Pallas kernels: none -> 473 us  [on_device(): pl.pallas_call(functools.partial(relay_kernel, ns, nb, hs, nc), out_shape...]
    select_n x152 -> x1, other arithmetic: 245 us -> 1.23 us  [on_device(): from_below = jnp.where(s == ns - 1, own[0], passed_along(own[1], -1))]
    dot_general x40 -> x0, matrix products: 211 us -> none  [the longest x38 195 us: backward_pass(): lax.dot_general(gathered, rows, (((1,), (1,)), ((), ())), preferred_eleme...]
    all_to_all x40 -> x1, waiting for transfers between devices: 203 us -> 0.01 us  [on_device(): lax.all_to_all(own.reshape(2, rows, 2, nb, hs), 'dp', split_axis=3, conca...]
    all_to_all x40 -> x1, starting transfers between devices: 145 us -> 6.32 us  [on_device(): lax.all_to_all(own.reshape(2, rows, 2, nb, hs), 'dp', split_axis=3, conca...]
    ppermute x38 -> x2, starting transfers between devices: 83.5 us -> 6.12 us  [passed_along(): return lax.ppermute(value, 'section', pairs)]
    psum x1 -> x0, blocking collectives: 66.8 us -> none  [on_device(): total = lax.psum(local_sum, ('section', 'dp'))]
  transfers between devices with their start and end apart: 116 -> 5, of which waited for: 114 -> 3; matrix products, arithmetic and copies ran while one was open for 8% -> 8% of each run, Pallas kernels for 0% -> 0%
where the time goes in v1:
time: 632 us; the launch traced here: 631 us
  Pallas kernels  473 us (75%)
  local copies, waits for them, and re-layouts  50.6 us (8%)
  waiting for transfers between devices  32.3 us (5%)
  blocking collectives  26.8 us (4%)
  other arithmetic  18.8 us (3%)
  between operations  16.7 us (3%)
  starting transfers between devices  12.5 us (2%)
    pallas_call x1, Pallas kernels, on_device(): pl.pallas_call(functools.partial(relay_kernel, ns, nb, hs, nc), out_shape...  473 us
    all_gather x1, blocking collectives, on_device(): scale = lax.all_gather(scale, 'dp', axis=1, tiled=True)[..., None]  26.8 us
    unnamed x19, local copies, waits for them, and re-layouts  18 us
    ppermute x2, waiting for transfers between devices, passed_along(): return lax.ppermute(value, 'section', pairs)  17.5 us
    all_gather x1, waiting for transfers between devices, on_device(): lax.all_gather(blocked(jnp.stack([from_above, from_below])), 'dp', axis=1...  14.7 us
    another operation x1, local copies, waits for them, and re-layouts, on_device(): wt = weights[::-1, 0].reshape(2, hs, 2, nb, hs).transpose(0, 3, 2, 4, 1)  13.5 us
  transfers between devices with their start and end apart: 5, of which 3 were waited for; matrix products, arithmetic and copies ran while one was open for 8% of the time, Pallas kernels for 0%

profile of v1, /device:TPU:1, one launch (start us, length us, event | category | flops | bytes accessed | tf_op | source)
XLA Modules:
  0.0 630.8 jit_solution(14109132138981091609)
XLA Ops:
  7.2 0.0 all-gather.6.cloned.1.call-start
  7.2 1.2 copy.41
  8.5 0.8 copy.45
  9.2 0.5 squeeze_reshape.3
  9.7 0.0 copy-start
  9.7 1.0 pad.4
  10.8 0.0 all-gather.6.cloned.1.call-update
  10.8 0.0 all-gather.4.cloned.1.call-start
  10.8 0.6 copy-done
  11.5 0.1 fusion.8
  11.6 4.8 collective-permute-start
  16.5 1.3 collective-permute-start.1
  17.8 14.0 %collective-permute-done = bf16[64,6144]{1,0:T(8,128)(2,1)} collective-permute-done((bf16[64,6144]{1,0:T(8,128)(2,1)S(1)}, bf16[64,6144]{1,0:T(8,128)(2,1)}, u32[]{:S(2)}, u32[]{:S(2)}) %collective-permute-start) | collective-permute-done | bytes 786464 | tf_op jit(solution)/shard_map/ppermute | solution.py:302
  31.8 1.3 copy.39
  33.0 3.5 collective-permute-done.1
  36.5 1.2 broadcast_select_fusion
  37.8 0.1 copy.40
  37.9 0.2 maximum_bitcast_fusion
  38.1 1.6 copy.23
  39.7 2.0 reshape.129
  41.7 0.0 all-gather.4.cloned.1.call-update
  41.7 0.1 rev.7
  41.8 0.3 copy.42
  42.1 2.6 copy.26
  44.7 6.3 %all-to-all-start = ((bf16[2,64,2,8,384]{4,2,1,0,3:T(2,128)(2,1)}), bf16[2,64,2,8,384]{4,2,1,0,3:T(2,128)(2,1)S(1)}, u32[]{:S(2)}, u32[]{:S(2)}) async-start(bf16[2,64,2,8,384]{4,2,1,0,3:T(2,128)(2,1)} %copy.26), calls=%async_computation | async-start | bytes 3145728 | tf_op jit(solution)/shard_map/all_to_all | solution.py:334
  51.1 0.4 multiply_reduce_fusion
  51.5 26.8 %all-gather = f32[8,64,2]{1,2,0:T(2,128)S(1)} all-gather(f32[1,64,2]{1,2,0:T(2,128)S(1)} %rsqrt_bitcast_fusion), channel_id=1, replica_groups=mesh['section'=16,'dp'=8] {'dp'}, dimensions={0}, use_global_device_ids=true | all-gather | bytes 4608 | tf_op jit(solution)/shard_map/all_gather | solution.py:333
  78.2 0.1 reshape.135
  78.3 0.1 mul.172
  78.4 0.1 mul.163
  78.5 10.0 %rev.6 = bf16[2,1,384,6144]{3,2,1,0:T(8,128)(2,1)} reverse(bf16[2,1,384,6144]{3,2,1,0:T(8,128)(2,1)} %param.5), dimensions={0} | reverse | bytes 18874368 | tf_op jit(solution)/shard_map/rev | solution.py:350
  88.5 9.9 %copy.38 = bf16[96,8,16,384]{3,2,1,0:T(8,128)(2,1)} copy(bf16[96,8,16,384]{3,1,2,0:T(8,128)(2,1)} %bitcast.83) | data formatting | bytes 18874368
  98.4 13.5 %copy.22 = bf16[2,384,2,8,384]{1,4,2,3,0:T(8,128)(2,1)} copy(bf16[2,384,2,8,384]{4,3,2,1,0:T(8,128)(2,1)} %bitcast.82) | data formatting | bytes 18874368 | tf_op jit(solution)/shard_map/reshape;squeeze | solution.py:350
  111.9 0.0 all-to-all-done
  111.9 0.5 bitcast_convert_fusion
  112.4 0.2 fusion.7
  112.6 1.6 copy.35
  114.3 1.6 copy.34
  115.9 0.9 multiply_multiply_fusion.1
  116.8 2.8 pad_maximum_fusion.coef
  119.6 0.3 copy-done.2
  119.9 1.4 fusion.6.h_t
  121.3 14.7 %all-gather.4.cloned.1.call-done.xp_hbm = bf16[2,16,8,32,768]{4,3,2,1,0:T(8,128)(2,1)} async-done(((bf16[2,2,8,32,768]{4,3,2,1,0:T(8,128)(2,1)}), bf16[2,16,8,32,768]{4,3,2,1,0:T(8,128)(2,1)}) %all-gather.4.cloned.1.call-update) | async-done | bytes 12582928 | tf_op jit(solution)/shard_map/all_gather | solution.py:325
  136.0 473.1 %relay.1 = (bf16[2,1,384,6144]{3,2,1,0:T(8,128)(2,1)}, bf16[64,6144]{1,0:T(8,128)(2,1)}, f32[2,8,128]{2,1,0:T(8,128)}) custom-call(bf16[2,8,768,384]{3,2,1,0:T(8,128)(2,1)} %bitcast.84, bf16[2,16,8,32,768]{4,3,2,1,0:T(8,128)(2,1)} %all-gather.4.cloned.1.call-done.xp_hbm, bf16[16,8,32,896]{3,2,1,0:T(8,128)(2,1)} %all-gather.6.cloned.1.call-done.cot_hbm, ...), custom_call_target="tpu_custom_call" | custom-call | tf_op jit(solution)/shard_map/relay/pallas_call | solution.py:356
  609.1 1.3 slice_reduce_fusion
  611.7 0.0 copy-start.4
  611.8 10.2 %multiply_convert_fusion = bf16[2,1,384,6144]{3,2,1,0:T(8,128)(2,1)} fusion(bf16[2,1,384,6144]{3,2,1,0:T(8,128)(2,1)} %get-tuple-element.7, f32[]{:T(128)S(6)} %min.3), kind=kLoop, calls=%fused_computation | loop fusion | flops 14155776 | bytes 18874372 | tf_op jit(solution)/shard_map/convert_element_type | solution.py:396
  621.9 0.9 copy.47
  (10 shorter events, 0.0 us)
Async XLA Ops:
  7.2 114.1 %all-gather.6.cloned.1.call-start = ((), (), s32[]{:S(2)}) async-start(), calls=%async_computation.2 | async-start | bytes 8257536 | tf_op jit(solution)/shard_map/all_gather | solution.py:330
  9.7 1.7 copy-start
  10.8 125.2 %all-gather.4.cloned.1.call-start = ((), (), s32[]{:S(2)}) async-start(), calls=%async_computation.1 | async-start | bytes 14155776 | tf_op jit(solution)/shard_map/all_gather | solution.py:325
  11.6 26.2 %copy-start.3 = (bf16[1,1,4,16,6144]{4,3,2,1,0:T(8,128)(2,1)}, bf16[1,1,4,16,6144]{4,3,2,1,0:T(8,128)(2,1)S(1)}, u32[]{:S(2)}) copy-start(bf16[1,1,4,16,6144]{4,3,2,1,0:T(8,128)(2,1)S(1)} %get-tuple-element.17) | copy-start | bytes 2359300
  11.6 20.1 %collective-permute-start = (bf16[64,6144]{1,0:T(8,128)(2,1)S(1)}, bf16[64,6144]{1,0:T(8,128)(2,1)}, u32[]{:S(2)}, u32[]{:S(2)}) collective-permute-start(bf16[64,6144]{1,0:T(8,128)(2,1)S(1)} %bitcast.93), channel_id=1, source_target_pairs={{0,8},{8,16},{16,24},{24,32},{32,40},{40,48},{48,56},{56,64},{64,7... | collective-permute-start | bytes 2359304 | tf_op jit(solution)/shard_map/ppermute | solution.py:302
  16.5 20.1 %collective-permute-start.1 = (bf16[64,6144]{1,0:T(8,128)(2,1)S(1)}, bf16[64,6144]{1,0:T(8,128)(2,1)}, u32[]{:S(2)}, u32[]{:S(2)}) collective-permute-start(bf16[64,6144]{1,0:T(8,128)(2,1)S(1)} %bitcast.98), channel_id=1, source_target_pairs={{8,0},{16,8},{24,16},{32,24},{40,32},{48,40},{56,48},{64,56},{72,6... | collective-permute-start | bytes 2359304 | tf_op jit(solution)/shard_map/ppermute | solution.py:302
  44.7 67.2 %all-to-all-start = ((bf16[2,64,2,8,384]{4,2,1,0,3:T(2,128)(2,1)}), bf16[2,64,2,8,384]{4,2,1,0,3:T(2,128)(2,1)S(1)}, u32[]{:S(2)}, u32[]{:S(2)}) async-start(bf16[2,64,2,8,384]{4,2,1,0,3:T(2,128)(2,1)} %copy.26), calls=%async_computation | async-start | bytes 3145728 | tf_op jit(solution)/shard_map/all_to_all | solution.py:334
  116.8 2.8 copy-start.1
  116.8 3.1 copy-start.2
  611.7 10.2 %copy-start.4 = (bf16[64,6144]{1,0:T(8,128)(2,1)S(1)}, bf16[64,6144]{1,0:T(8,128)(2,1)}, u32[]{:S(2)}) copy-start(bf16[64,6144]{1,0:T(8,128)(2,1)} %get-tuple-element.6) | copy-start | bytes 2359300
Sparse Core Ops, SparseCore 0:
  10.9 54.0 all-gather.5
  66.6 69.3 all-gather.3

commit v2 on v1

--- a/solution.py
+++ b/solution.py
@@ -11,37 +11,38 @@
 MESH = pl.DeviceIdType.MESH
 T = 32
 LAG = (3, 5)
+QROWS = 256
 
 
 def relay_kernel(
-    ns, nb, hs, nc, wt_hbm, xp_hbm, cot_hbm, coef, h_t, x_own,
+    ns, nb, hs, nc, w_hbm, x_hbm, cot_hbm,
     grads, leaving, stats,
-    wt, xg, u, q, sbuf, obuf, gtile, stat_dp, stat_sec, stat_me,
-    recv, relay_sem, send_sem, own_send, own_recv, load_sem, tile_sem, stat_send, stat_recv,
+    wt, xg, u, q, coef, feats, feats_t, sbuf, obuf, gtile, wpart, xrows, xs, rbuf,
+    stat_dp, stat_sec, stat_me,
+    recv, relay_sem, send_sem, own_send, own_recv, tile_sem, stat_send, stat_recv,
+    w_sem, row_sem, xs_recv, xs_send, xs_own, r_recv, r_send, hop_send, x_recv, x_send,
 ):
-    f32 = jnp.float32
+    f32, bf16 = jnp.float32, jnp.bfloat16
     s = lax.axis_index("section")
     me = lax.axis_index("dp")
     y = lax.div(me, 2)
     c = lax.rem(me, 2)
     ny = nb // 2
+    half_width = nb * hs
     partner = me + 1 - 2 * c
     per_owner = nc // nb
-    wide = 2 * hs + 128
-
-    loads = []
-    for leg in range(2):
-        loads.append(pltpu.make_async_copy(wt_hbm.at[leg], wt.at[leg], load_sem.at[leg, 0]))
-        loads.append(pltpu.make_async_copy(xp_hbm.at[leg], xg.at[leg], load_sem.at[leg, 1]))
-    for copy in loads:
-        copy.start()
+    rows = per_owner * T
+
+    def at(section, dp):
+        return {"section": section, "dp": dp}
 
     barrier = pltpu.get_barrier_semaphore()
 
     def greet(section, dp):
-        pl.semaphore_signal(
-            barrier, inc=1, device_id={"section": section, "dp": dp}, device_id_type=MESH
-        )
+        pl.semaphore_signal(barrier, inc=1, device_id=at(section, dp), device_id_type=MESH)
+
+    row_copy = pltpu.make_async_copy(x_hbm, xrows, row_sem)
+    row_copy.start()
 
     for j in range(1, nb):
         greet(s, lax.rem(me + j, nb))
@@ -62,34 +63,179 @@
         barrier, nb - 1 + ns - 1 + ny * jnp.where(s < ns - 1, 1, 0) + ny * jnp.where(s > 0, 1, 0)
     )
 
+    own_rows = pl.ds(per_owner * me, per_owner)
+
+    def remote(src, dst, send, recv, section, dp):
+        return pltpu.make_async_remote_copy(
+            src_ref=src, dst_ref=dst, send_sem=send, recv_sem=recv,
+            device_id=at(section, dp), device_id_type=MESH,
+        )
+
+    def send_slices(leg):
+        for j in range(1, nb):
+            dp = lax.rem(me + j, nb)
+            for part in range(2):
+                columns = pl.ds(pl.multiple_of(part * half_width + dp * hs, 128), hs)
+                remote(
+                    x_hbm.at[1 - leg, :, :, columns], xs.at[leg, me, :, :, pl.ds(part * hs, hs)],
+                    xs_send.at[leg], xs_recv.at[leg], s, dp,
+                ).start()
+        for part in range(2):
+            columns = pl.ds(pl.multiple_of(part * half_width + me * hs, 128), hs)
+            pltpu.make_async_copy(
+                x_hbm.at[1 - leg, :, :, columns], xs.at[leg, me, :, :, pl.ds(part * hs, hs)],
+                xs_own.at[leg],
+            ).start()
+
+    def send_rows():
+        @pl.when(s < ns - 1)
+        def _():
+            remote(
+                x_hbm.at[1], xg.at[0, own_rows], hop_send.at[0], x_recv.at[0, me], s + 1, me
+            ).start()
+
+        @pl.when(s == 0)
+        def _():
+            pltpu.make_async_copy(cot_hbm, xg.at[0, own_rows], x_recv.at[0, me]).start()
+
+        @pl.when(s > 0)
+        def _():
+            remote(
+                x_hbm.at[0], xg.at[1, own_rows], hop_send.at[1], x_recv.at[1, me], s - 1, me
+            ).start()
+
+        @pl.when(s == ns - 1)
+        def _():
+            pltpu.make_async_copy(x_hbm.at[1], xg.at[1, own_rows], x_recv.at[1, me]).start()
+
+    def send_scales(leg):
+        total = jnp.zeros((per_owner, T, 128), f32)
+        for lane in range(0, 2 * half_width, 128):
+            value = xrows[1 - leg, :, :, lane : lane + 128].astype(f32)
+            total += value * value
+        mean = jnp.sum(total, axis=-1, keepdims=True) / (2 * half_width)
+        rbuf[leg, me] = jnp.broadcast_to(lax.rsqrt(mean + epsilon), (per_owner, T, 128))
+        for j in range(1, nb):
+            remote(
+                rbuf.at[leg, me], rbuf.at[leg, me], r_send.at[leg], r_recv.at[leg],
+                s, lax.rem(me + j, nb),
+            ).start()
+
+    def rows_here(leg, owner):
+        block = xg.at[leg, pl.ds(per_owner * owner, per_owner)]
+        pltpu.make_async_copy(block, block, x_recv.at[leg, owner]).wait()
+        return block
+
+    def spread_rows(leg):
+        block = rows_here(leg, me)
+        for dy in (2, 1, 3):
+            dp = 2 * lax.rem(y + dy, ny) + c
+            remote(block, block, x_send.at[leg], x_recv.at[leg, me], s, dp).start()
+        remote(block, block, x_send.at[leg], x_recv.at[leg, me], s, partner).start()
+
+    def relay_rows(leg):
+        for dy in (3, 1, 2):
+            owner = 2 * lax.rem(y + dy, ny) + c
+            block = rows_here(leg, owner)
+            remote(block, block, x_send.at[leg], x_recv.at[leg, owner], s, partner).start()
+
+    def transpose_weight(leg):
+        def piece(j, slot):
+            return pltpu.make_async_copy(
+                w_hbm.at[1 - leg, 0, :, pl.ds(j * 2 * hs, 2 * hs)], wpart.at[slot], w_sem.at[slot]
+            )
+
+        piece(0, 0).start()
+        for j in range(nb):
+            slot = j % 2
+            if j + 1 < nb:
+                piece(j + 1, 1 - slot).start()
+            piece(j, slot).wait()
+            for i in range(2):
+                column = 2 * j + i
+                part, b = column // nb, column % nb
+                wt[leg, b, part * hs : (part + 1) * hs, :] = wpart[slot, :, i * hs : (i + 1) * hs].T
+
+    def local_factors(leg):
+        some = xs.at[leg, pl.ds(0, nb - 1)]
+        pltpu.make_async_copy(some, some, xs_recv.at[leg]).wait()
+        one = xs.at[leg, 0]
+        pltpu.make_async_copy(one, one, xs_own.at[leg]).wait()
+        some = rbuf.at[leg, pl.ds(0, nb - 1)]
+        pltpu.make_async_copy(some, some, r_recv.at[leg]).wait()
+
+        def chunk(k, _):
+            owner, half = lax.div(k, per_owner), lax.rem(k, per_owner)
+            scale = jnp.concatenate([rbuf[leg, owner, half]] * (hs // 128), axis=1)
+            value = xs[leg, owner, half].astype(f32)
+            first = value[:, :hs] * scale
+            gate_in = value[:, hs:] * scale
+            gated = jax.nn.sigmoid(gate_in)
+            feat = first * gated
+            coef[leg, 0, k] = scale * gated
+            coef[leg, 1, k] = scale * feat * (1.0 - gated)
+            coef[leg, 2, k] = (
+                scale * scale * feat * (1.0 + (1.0 - gated) * gate_in) / (2 * half_width)
+            )
+            feats[leg, k] = feat.astype(bf16)
+            return 0
+
+        lax.fori_loop(0, nc, chunk, 0)
+
+    def columns_of(b, part):
+        return pl.ds(part * half_width + b * hs, hs)
+
+    def fill_q(leg):
+        for dy in range(ny):
+            rows_here(leg, 2 * lax.rem(y + dy, ny) + 1 - c)
+        group = QROWS // T
+
+        def fill(i, _):
+            ks = pl.ds(i * group, group)
+            total = jnp.zeros((QROWS, hs), f32)
+            for b in range(nb):
+                both = [xg[leg, ks, :, columns_of(b, part)].reshape(QROWS, hs) for part in range(2)]
+                total += jnp.dot(
+                    jnp.concatenate(both, axis=1), wt[leg, b], preferred_element_type=f32
+                )
+            q[leg, ks] = total.reshape(group, T, hs)
+            return 0
+
+        lax.fori_loop(0, nc // group, fill, 0)
+        some = xg.at[leg, pl.ds(0, per_owner * (nb - 1))]
+        pltpu.make_async_copy(some, some, x_send.at[leg]).wait()
+
+    send_slices(0)
+    send_rows()
+    row_copy.wait()
+    send_scales(0)
+    spread_rows(0)
+    send_slices(1)
+    send_scales(1)
+
     @pl.when(s == 0)
     def _():
-        copy = pltpu.make_async_copy(cot_hbm, u.at[0], load_sem.at[0, 2])
-        copy.start()
-        copy.wait()
-
-    for copy in loads:
-        copy.wait()
-
-    for leg in range(2):
-        def fill(k, _, leg=leg):
-            total = jnp.zeros((T, hs), f32)
+        def clear(k, _):
             for b in range(nb):
-                total += jnp.dot(xg[leg, k, b], wt[leg, b], preferred_element_type=f32)
-            q[leg, k] = total
+                u[0, k, b, :, : 2 * hs] = jnp.zeros((T, 2 * hs), bf16)
+                u[0, k, b, :, 2 * hs :] = jnp.full((T, 128), -1.0 if b == 0 else 0.0, bf16)
             return 0
 
-        lax.fori_loop(0, nc, fill, 0)
+        lax.fori_loop(0, nc, clear, 0)
+
+    transpose_weight(0)
+    relay_rows(0)
+    local_factors(0)
+    fill_q(0)
 
     def step(leg, k):
-        first = (s == 0) if leg == 0 else False
         acc = jnp.zeros((T, hs), f32)
 
         def arrived(b):
             block = u.at[leg, k, b]
             pltpu.make_async_copy(block, block, recv.at[leg, k, b]).wait()
 
-        for dy in (0, 1, 3, 2):
+        for dy in (2, 3, 1, 0):
             b = 2 * lax.rem(y + dy, ny) + c
 
             def pass_on(b=b):
@@ -108,7 +254,7 @@
             else:
                 pass_on()
             acc += jnp.dot(u[leg, k, b][:, : 2 * hs], wt[leg, b], preferred_element_type=f32)
-        for dy in (0, 1, 3, 2):
+        for dy in (2, 3, 1, 0):
             b = 2 * lax.rem(y + dy, ny) + 1 - c
             if leg == 0:
                 pl.when(s > 0)(functools.partial(arrived, b))
@@ -121,9 +267,12 @@
         kap = jnp.concatenate([kap] * (hs // 128), axis=1)
         dh = acc - kap * q[leg, k]
         mine = u[leg, k, me].astype(f32)
-        x_mine = xg[leg, k, me].astype(f32)
-        new_a = mine[:, :hs] - kap * x_mine[:, :hs] + coef[leg, 0, k] * dh
-        new_g = mine[:, hs : 2 * hs] - kap * x_mine[:, hs:] + coef[leg, 1, k] * dh
+        x_mine = [
+            xg[leg, k, :, pl.ds(pl.multiple_of(part * half_width + me * hs, 128), hs)].astype(f32)
+            for part in range(2)
+        ]
+        new_a = mine[:, :hs] - kap * x_mine[0] + coef[leg, 0, k] * dh
+        new_g = mine[:, hs : 2 * hs] - kap * x_mine[1] + coef[leg, 1, k] * dh
         part = jnp.sum(coef[leg, 2, k] * dh, axis=1, keepdims=True)
         sbuf[leg, k, :, :hs] = new_a.astype(jnp.bfloat16)
         sbuf[leg, k, :, hs : 2 * hs] = new_g.astype(jnp.bfloat16)
@@ -174,32 +323,18 @@
                     device_id_type=MESH,
                 ).start()
 
-        wide_kap = jnp.concatenate([kap, kap], axis=1)
         for b in range(nb):
-            value = u[leg, k, b][:, : 2 * hs].astype(f32) - wide_kap * xg[leg, k, b].astype(f32)
-            xg[leg, k, b] = value.astype(jnp.bfloat16)
-
-    lag = jnp.minimum(nc, LAG[0] + LAG[1] * (ns - 1 - s))
-
-    def advance(i, _):
-        @pl.when(i < nc)
-        def _():
-            step(0, i)
-
-        @pl.when(i >= lag)
-        def _():
-            step(1, i - lag)
-
-        return 0
-
-    lax.fori_loop(0, nc + lag, advance, 0)
-
-    stat_me[...] = jnp.zeros_like(stat_me)
-    for leg in range(2):
-        def tile(j, _, leg=leg):
+            for part in range(2):
+                value = u[leg, k, b, :, part * hs : (part + 1) * hs].astype(f32)
+                value -= kap * xg[leg, k, :, columns_of(b, part)].astype(f32)
+                xg[leg, k, :, columns_of(b, part)] = value.astype(bf16)
+
+    def weight_grad(leg):
+        feats_t[...] = feats[leg].reshape(nc * T, hs).T
+
+        def tile(j, _):
             slot = lax.rem(j, 2)
-            b = lax.div(j, 2)
-            columns = pl.ds(pl.multiple_of(slot * nb * hs + b * hs, 128), hs)
+            columns = pl.ds(pl.multiple_of(j * hs, 128), hs)
             copy = pltpu.make_async_copy(
                 gtile.at[slot], grads.at[1 - leg, 0, :, columns], tile_sem.at[slot]
             )
@@ -208,10 +343,9 @@
             def _():
                 copy.wait()
 
-            offset = pl.multiple_of(slot * hs, 128)
-            right = xg[leg, :, b, :, pl.ds(offset, hs)].reshape(nc * T, hs)
-            out = jnp.dot(h_t[leg], right, preferred_element_type=f32)
-            gtile[slot] = out.astype(jnp.bfloat16)
+            right = xg[leg, :, :, columns].reshape(nc * T, hs)
+            out = jnp.dot(feats_t[...], right, preferred_element_type=f32)
+            gtile[slot] = out.astype(bf16)
             copy.start()
             folded = out.reshape(hs // 8, 8, hs)
             squares = jnp.sum(folded * folded, axis=0)
@@ -226,6 +360,38 @@
             pltpu.make_async_copy(
                 gtile.at[slot], grads.at[1 - leg, 0, :, pl.ds(0, hs)], tile_sem.at[slot]
             ).wait()
+
+    stat_me[...] = jnp.zeros_like(stat_me)
+    lag = jnp.minimum(nc, LAG[0] + LAG[1] * (ns - 1 - s))
+    early = lag < nc
+    prepare_at = jnp.where(early, 0, nc)
+    grad_at = jnp.where(early, nc + lag, nc)
+
+    def advance(i, _):
+        @pl.when(i == prepare_at)
+        def _():
+            spread_rows(1)
+            relay_rows(1)
+            transpose_weight(1)
+            local_factors(1)
+            fill_q(1)
+
+        @pl.when(i == grad_at)
+        def _():
+            weight_grad(0)
+
+        @pl.when(i < nc)
+        def _():
+            step(0, i)
+
+        @pl.when((i >= lag) & (i < nc + lag))
+        def _():
+            step(1, i - lag)
+
+        return 0
+
+    lax.fori_loop(0, nc + lag + 1, advance, 0)
+    weight_grad(1)
 
     stat_dp[me] = stat_me[...]
     for j in range(1, nb):
@@ -252,13 +418,12 @@
             pltpu.make_async_copy(block, block, own_recv.at[half, b]).wait()
         kap = jnp.sum(obuf[half, :, :, 2 * hs :].astype(f32), axis=0)
         kap = jnp.concatenate([kap] * (hs // 128), axis=1)
-        rows = pl.ds(half * T, T)
         for b in range(nb):
             for part in range(2):
-                columns = pl.ds(part * nb * hs + b * hs, hs)
+                columns = columns_of(b, part)
                 value = obuf[half, b, :, part * hs : (part + 1) * hs].astype(f32)
-                value -= kap * x_own[rows, columns].astype(f32)
-                leaving[rows, columns] = value.astype(jnp.bfloat16)
+                value -= kap * xrows[0, half, :, columns].astype(f32)
+                leaving[half, :, columns] = value.astype(bf16)
 
     some = stat_sec.at[pl.ds(0, ns - 1)]
     pltpu.make_async_copy(some, some, stat_recv.at[1]).wait()
@@ -295,60 +460,31 @@
 
     lax.fori_loop(0, nc, drain, 0)
 
-
-def passed_along(value, by):
-    length = lax.axis_size("section")
-    pairs = [(i, i + by) for i in range(length) if 0 <= i + by < length]
-    return lax.ppermute(value, "section", pairs)
+    for leg in range(2):
+        some = xs.at[leg, pl.ds(0, nb - 1)]
+        pltpu.make_async_copy(some, some, xs_send.at[leg]).wait()
+        some = rbuf.at[leg, pl.ds(0, nb - 1)]
+        pltpu.make_async_copy(some, some, r_send.at[leg]).wait()
+    one = xg.at[0, pl.ds(0, per_owner)]
+
+    @pl.when(s < ns - 1)
+    def _():
+        pltpu.make_async_copy(one, one, hop_send.at[0]).wait()
+
+    @pl.when(s > 0)
+    def _():
+        pltpu.make_async_copy(one, one, hop_send.at[1]).wait()
 
 
 def on_device(cotangent, saved_inputs, weights):
     f32, bf16 = jnp.float32, jnp.bfloat16
     ns = lax.axis_size("section")
     nb = lax.axis_size("dp")
-    s = lax.axis_index("section")
     hs, width = weights.shape[2:]
     rows = saved_inputs.shape[2] * saved_inputs.shape[3]
     per_owner = rows // T
     nc = per_owner * nb
     wide = 2 * hs + 128
-
-    own = saved_inputs[:, 0].reshape(2, rows, width)[::-1]
-    from_above = passed_along(own[0], 1)
-    from_below = jnp.where(s == ns - 1, own[0], passed_along(own[1], -1))
-
-    def blocked(value):
-        legs = value.shape[0]
-        value = value.reshape(legs, per_owner, T, 2, nb, hs)
-        return value.transpose(0, 1, 4, 2, 3, 5).reshape(legs, per_owner, nb, T, 2 * hs)
-
-    before = lax.all_gather(
-        blocked(jnp.stack([from_above, from_below])), "dp", axis=1, tiled=True
-    )
-    start = blocked(cotangent.reshape(1, rows, width))[0]
-    start = jnp.pad(start, ((0, 0), (0, 0), (0, 0), (0, 128)))
-    start = lax.all_gather(start, "dp", axis=0, tiled=True)
-
-    scale = lax.rsqrt(jnp.mean(jnp.square(own.astype(f32)), axis=-1) + epsilon)
-    scale = lax.all_gather(scale, "dp", axis=1, tiled=True)[..., None]
-    mine = lax.all_to_all(
-        own.reshape(2, rows, 2, nb, hs), "dp", split_axis=3, concat_axis=1, tiled=True
-    )[:, :, :, 0].astype(f32)
-    first = mine[:, :, 0] * scale
-    gate_in = mine[:, :, 1] * scale
-    gated = jax.nn.sigmoid(gate_in)
-    feats = first * gated
-    coef = jnp.stack(
-        [
-            scale * gated,
-            scale * feats * (1.0 - gated),
-            scale * scale * feats * (1.0 + (1.0 - gated) * gate_in) / width,
-        ],
-        axis=1,
-    ).reshape(2, 3, nc, T, hs)
-    h_t = feats.astype(bf16).transpose(0, 2, 1)
-    wt = weights[::-1, 0].reshape(2, hs, 2, nb, hs).transpose(0, 3, 2, 4, 1)
-    wt = wt.reshape(2, nb, 2 * hs, hs)
 
     vmem = pl.BlockSpec(memory_space=pltpu.VMEM)
     hbm = pl.BlockSpec(memory_space=pl.ANY)
@@ -357,19 +493,26 @@
         functools.partial(relay_kernel, ns, nb, hs, nc),
         out_shape=(
             jax.ShapeDtypeStruct((2, 1, hs, width), bf16),
-            jax.ShapeDtypeStruct((rows, width), bf16),
+            jax.ShapeDtypeStruct((per_owner, T, width), bf16),
             jax.ShapeDtypeStruct((2, 8, 128), f32),
         ),
-        in_specs=[hbm, hbm, hbm, vmem, vmem, vmem],
+        in_specs=[hbm, hbm, hbm],
         out_specs=(hbm, vmem, vmem),
         scratch_shapes=[
             pltpu.VMEM((2, nb, 2 * hs, hs), bf16),
-            pltpu.VMEM((2, nc, nb, T, 2 * hs), bf16),
+            pltpu.VMEM((2, nc, T, width), bf16),
             pltpu.VMEM((2, nc, nb, T, wide), bf16),
             pltpu.VMEM((2, nc, T, hs), f32),
+            pltpu.VMEM((2, 3, nc, T, hs), f32),
+            pltpu.VMEM((2, nc, T, hs), bf16),
+            pltpu.VMEM((hs, nc * T), bf16),
             pltpu.VMEM((2, nc, T, wide), bf16),
             pltpu.VMEM((per_owner, nb, T, wide), bf16),
             pltpu.VMEM((2, hs, hs), bf16),
+            pltpu.VMEM((2, hs, 2 * hs), bf16),
+            pltpu.VMEM((2, per_owner, T, width), bf16),
+            pltpu.VMEM((2, nb, per_owner, T, 2 * hs), bf16),
+            pltpu.VMEM((2, nb, per_owner, T, 128), f32),
             pltpu.VMEM((nb, 2, 8, 128), f32),
             pltpu.VMEM((ns, 2, 8, 128), f32),
             pltpu.VMEM((2, 8, 128), f32),
@@ -378,16 +521,29 @@
             dma((2, nc)),
             dma((nc,)),
             dma((per_owner, nb)),
-            dma((2, 3)),
-            dma((2,)),
-            dma((2,)),
+            dma((2,)),
+            dma((2,)),
+            dma((2,)),
+            dma((2,)),
+            dma,
+            dma((2,)),
+            dma((2,)),
+            dma((2,)),
+            dma((2,)),
+            dma((2,)),
+            dma((2,)),
+            dma((2, nb)),
             dma((2,)),
         ],
         compiler_params=pltpu.CompilerParams(
-            collective_id=0, has_side_effects=True, vmem_limit_bytes=58 * 2**20
+            collective_id=0, has_side_effects=True, vmem_limit_bytes=60 * 2**20
         ),
         name="relay",
-    )(wt, before, start, coef, h_t, own[1])
+    )(
+        weights,
+        saved_inputs.reshape(2, per_owner, T, width),
+        cotangent.reshape(per_owner, T, width),
+    )
 
     total = jnp.sum(stats[0])
     largest = jnp.max(stats[1])

time: 632 us -> 554 us (0.88)
  Pallas kernels: 473 us -> 538 us
  local copies, waits for them, and re-layouts: 50.6 us -> 0.88 us
  waiting for transfers between devices: 32.3 us -> 0 us
  blocking collectives: 26.8 us -> 0 us
  between operations: 16.7 us -> 3.12 us
  starting transfers between devices: 12.5 us -> 0 us
  other arithmetic: 18.8 us -> 11.5 us
    pallas_call x1, Pallas kernels: 473 us -> 538 us  [on_device(): pl.pallas_call(functools.partial(relay_kernel, ns, nb, hs, nc), out_shape...]
    all_gather x1 -> x0, blocking collectives: 26.8 us -> none  [on_device(): scale = lax.all_gather(scale, 'dp', axis=1, tiled=True)[..., None]]
    ppermute x2 -> x0, waiting for transfers between devices: 17.5 us -> none  [passed_along(): return lax.ppermute(value, 'section', pairs)]
    unnamed x19 -> x3, local copies, waits for them, and re-layouts: 18 us -> 0.88 us
    another operation x3 -> x0, local copies, waits for them, and re-layouts: 14.8 us -> none  [the longest x1 13.5 us: on_device(): wt = weights[::-1, 0].reshape(2, hs, 2, nb, hs).transpose(0, 3, 2, 4, 1)]
    all_gather x2 -> x0, waiting for transfers between devices: 14.7 us -> none  [the longest x1 14.7 us: on_device(): lax.all_gather(blocked(jnp.stack([from_above, from_below])), 'dp', axis=1...]
    rev x2 -> x0, local copies, waits for them, and re-layouts: 10.2 us -> none  [the longest x1 10 us: on_device(): wt = weights[::-1, 0].reshape(2, hs, 2, nb, hs).transpose(0, 3, 2, 4, 1)]
    all_to_all x1 -> x0, starting transfers between devices: 6.32 us -> none  [on_device(): lax.all_to_all(own.reshape(2, rows, 2, nb, hs), 'dp', split_axis=3, conca...]
  transfers between devices with their start and end apart: 5 -> 0, of which waited for: 3 -> 0; matrix products, arithmetic and copies ran while one was open for 8% -> 0% of each run, Pallas kernels for 0% -> 0%
where the time goes in v2:
time: 554 us
  Pallas kernels  538 us (97%)
  other arithmetic  11.5 us (2%)
    pallas_call x1, Pallas kernels, on_device(): pl.pallas_call(functools.partial(relay_kernel, ns, nb, hs, nc), out_shape...  538 us

profile of v2, /device:TPU:1, one launch (start us, length us, event | category | flops | bytes accessed | tf_op | source)
XLA Modules:
  0.0 553.6 jit_solution(17409150396109547278)
XLA Ops:
  0.6 538.1 %relay.1 = (bf16[2,1,384,6144]{3,2,1,0:T(8,128)(2,1)}, bf16[2,32,6144]{2,1,0:T(8,128)(2,1)}, f32[2,8,128]{2,1,0:T(8,128)}) custom-call(bf16[2,1,384,6144]{3,2,1,0:T(8,128)(2,1)} %w_hbm.1, bf16[2,2,32,6144]{3,2,1,0:T(8,128)(2,1)} %bitcast.3, bf16[2,32,6144]{2,1,0:T(8,128)(2,1)} %bitcast.4), custom_call_target="tpu_custom_call" | custom-call | tf_op jit(solution)/shard_map/relay/pallas_call | solution.py:492
  538.8 1.3 slice_reduce_fusion
  541.4 0.0 copy-start
  541.4 10.2 %multiply_convert_fusion = bf16[2,1,384,6144]{3,2,1,0:T(8,128)(2,1)} fusion(bf16[2,1,384,6144]{3,2,1,0:T(8,128)(2,1)} %get-tuple-element.7, f32[]{:T(128)S(6)} %min_shard_map.3), kind=kLoop, calls=%fused_computation | loop fusion | flops 14155776 | bytes 18874372 | tf_op jit(solution)/shard_map/convert_element_type | solution.py:552
  551.6 0.0 copy-done
  551.6 0.9 copy.7
Async XLA Ops:
  541.4 10.2 %copy-start = (bf16[2,32,6144]{2,1,0:T(8,128)(2,1)S(1)}, bf16[2,32,6144]{2,1,0:T(8,128)(2,1)}, u32[]{:S(2)}) copy-start(bf16[2,32,6144]{2,1,0:T(8,128)(2,1)} %get-tuple-element.6) | copy-start | bytes 2359300

commit v3 on v2

--- a/solution.py
+++ b/solution.py
@@ -9,9 +9,13 @@
 
 epsilon = 1e-05
 MESH = pl.DeviceIdType.MESH
-T = 32
-LAG = (3, 5)
-QROWS = 256
+T = 16
+TAKE = 1
+LAG = (3, 7)
+LAZY = 3
+PREPARE = 9
+GRAD = 4
+DIRECT = (2, 0)
 
 
 def relay_kernel(
@@ -31,7 +35,6 @@
     half_width = nb * hs
     partner = me + 1 - 2 * c
     per_owner = nc // nb
-    rows = per_owner * T
 
     def at(section, dp):
         return {"section": section, "dp": dp}
@@ -62,8 +65,6 @@
     pl.semaphore_wait(
         barrier, nb - 1 + ns - 1 + ny * jnp.where(s < ns - 1, 1, 0) + ny * jnp.where(s > 0, 1, 0)
     )
-
-    own_rows = pl.ds(per_owner * me, per_owner)
 
     def remote(src, dst, send, recv, section, dp):
         return pltpu.make_async_remote_copy(
@@ -87,26 +88,22 @@
                 xs_own.at[leg],
             ).start()
 
-    def send_rows():
-        @pl.when(s < ns - 1)
-        def _():
-            remote(
-                x_hbm.at[1], xg.at[0, own_rows], hop_send.at[0], x_recv.at[0, me], s + 1, me
-            ).start()
-
-        @pl.when(s == 0)
-        def _():
-            pltpu.make_async_copy(cot_hbm, xg.at[0, own_rows], x_recv.at[0, me]).start()
-
-        @pl.when(s > 0)
-        def _():
-            remote(
-                x_hbm.at[0], xg.at[1, own_rows], hop_send.at[1], x_recv.at[1, me], s - 1, me
-            ).start()
-
-        @pl.when(s == ns - 1)
-        def _():
-            pltpu.make_async_copy(x_hbm.at[1], xg.at[1, own_rows], x_recv.at[1, me]).start()
+    def send_rows(leg):
+        for part in range(per_owner):
+            own = xg.at[leg, part * nb + me]
+            arrival = x_recv.at[leg, part, me]
+            ends = (s < ns - 1, s == 0) if leg == 0 else (s > 0, s == ns - 1)
+
+            @pl.when(ends[0])
+            def _():
+                remote(
+                    x_hbm.at[1 - leg, part], own, hop_send.at[leg], arrival, s + 1 - 2 * leg, me
+                ).start()
+
+            @pl.when(ends[1])
+            def _():
+                first = cot_hbm.at[part] if leg == 0 else x_hbm.at[1, part]
+                pltpu.make_async_copy(first, own, arrival).start()
 
     def send_scales(leg):
         total = jnp.zeros((per_owner, T, 128), f32)
@@ -121,23 +118,24 @@
                 s, lax.rem(me + j, nb),
             ).start()
 
-    def rows_here(leg, owner):
-        block = xg.at[leg, pl.ds(per_owner * owner, per_owner)]
-        pltpu.make_async_copy(block, block, x_recv.at[leg, owner]).wait()
+    def rows_here(leg, part, owner):
+        block = xg.at[leg, part * nb + owner]
+        pltpu.make_async_copy(block, block, x_recv.at[leg, part, owner]).wait()
         return block
 
-    def spread_rows(leg):
-        block = rows_here(leg, me)
+    def send_block(block, leg, part, owner, dp):
+        remote(block, block, x_send.at[leg, part], x_recv.at[leg, part, owner], s, dp).start()
+
+    def spread_rows(leg, part):
+        block = rows_here(leg, part, me)
         for dy in (2, 1, 3):
-            dp = 2 * lax.rem(y + dy, ny) + c
-            remote(block, block, x_send.at[leg], x_recv.at[leg, me], s, dp).start()
-        remote(block, block, x_send.at[leg], x_recv.at[leg, me], s, partner).start()
-
-    def relay_rows(leg):
+            send_block(block, leg, part, me, 2 * lax.rem(y + dy, ny) + c)
+        send_block(block, leg, part, me, partner)
+
+    def relay_rows(leg, part):
         for dy in (3, 1, 2):
             owner = 2 * lax.rem(y + dy, ny) + c
-            block = rows_here(leg, owner)
-            remote(block, block, x_send.at[leg], x_recv.at[leg, owner], s, partner).start()
+            send_block(rows_here(leg, part, owner), leg, part, owner, partner)
 
     def transpose_weight(leg):
         def piece(j, slot):
@@ -165,7 +163,7 @@
         pltpu.make_async_copy(some, some, r_recv.at[leg]).wait()
 
         def chunk(k, _):
-            owner, half = lax.div(k, per_owner), lax.rem(k, per_owner)
+            owner, half = lax.rem(k, nb), lax.div(k, nb)
             scale = jnp.concatenate([rbuf[leg, owner, half]] * (hs // 128), axis=1)
             value = xs[leg, owner, half].astype(f32)
             first = value[:, :hs] * scale
@@ -185,33 +183,30 @@
     def columns_of(b, part):
         return pl.ds(part * half_width + b * hs, hs)
 
-    def fill_q(leg):
+    def fill_q(leg, part):
         for dy in range(ny):
-            rows_here(leg, 2 * lax.rem(y + dy, ny) + 1 - c)
-        group = QROWS // T
-
-        def fill(i, _):
-            ks = pl.ds(i * group, group)
-            total = jnp.zeros((QROWS, hs), f32)
-            for b in range(nb):
-                both = [xg[leg, ks, :, columns_of(b, part)].reshape(QROWS, hs) for part in range(2)]
-                total += jnp.dot(
-                    jnp.concatenate(both, axis=1), wt[leg, b], preferred_element_type=f32
-                )
-            q[leg, ks] = total.reshape(group, T, hs)
-            return 0
-
-        lax.fori_loop(0, nc // group, fill, 0)
-        some = xg.at[leg, pl.ds(0, per_owner * (nb - 1))]
-        pltpu.make_async_copy(some, some, x_send.at[leg]).wait()
+            rows_here(leg, part, 2 * lax.rem(y + dy, ny) + 1 - c)
+        ks = pl.ds(part * nb, nb)
+        total = jnp.zeros((nb * T, hs), f32)
+        for b in range(nb):
+            both = [xg[leg, ks, :, columns_of(b, i)].reshape(nb * T, hs) for i in range(2)]
+            total += jnp.dot(
+                jnp.concatenate(both, axis=1), wt[leg, b], preferred_element_type=f32
+            )
+        q[leg, ks] = total.reshape(nb, T, hs)
+        some = xg.at[leg, pl.ds(0, nb - 1)]
+        pltpu.make_async_copy(some, some, x_send.at[leg, part]).wait()
 
     send_slices(0)
-    send_rows()
+    send_rows(0)
     row_copy.wait()
     send_scales(0)
-    spread_rows(0)
-    send_slices(1)
-    send_scales(1)
+    spread_rows(0, 0)
+
+    @pl.when(s >= LAZY)
+    def _():
+        for part in range(1, per_owner):
+            spread_rows(0, part)
 
     @pl.when(s == 0)
     def _():
@@ -224,42 +219,70 @@
         lax.fori_loop(0, nc, clear, 0)
 
     transpose_weight(0)
-    relay_rows(0)
+    relay_rows(0, 0)
     local_factors(0)
-    fill_q(0)
+    fill_q(0, 0)
+
+    @pl.when(s >= LAZY)
+    def _():
+        for part in range(1, per_owner):
+            relay_rows(0, part)
+            fill_q(0, part)
+
+    def arrived(leg, k, b):
+        block = u.at[leg, k, b]
+        pltpu.make_async_copy(block, block, recv.at[leg, k, b]).wait()
+
+    def pass_on(leg, k, b, dp):
+        block = u.at[leg, k, b]
+        remote(block, block, relay_sem.at[leg, k], recv.at[leg, k, b], s, dp).start()
+
+    def lane_mate(dy):
+        return 2 * lax.rem(y + dy, ny) + c
+
+    def other_lane(dy):
+        return lane_mate(dy) + 1 - 2 * c
+
+    def blocks(leg, k, count, semaphore):
+        some = u.at[leg, k, pl.ds(0, count)]
+        pltpu.make_async_copy(some, some, semaphore).wait()
+
+    def take(leg, k):
+        arrived(leg, k, me)
+        for dy in (1, 3):
+            for mate in (lane_mate(dy), other_lane(dy)):
+                pass_on(leg, k, me, mate)
+        pass_on(leg, k, me, partner)
+
+    def relay(leg, k):
+        arrived(leg, k, lane_mate(2))
+        pass_on(leg, k, lane_mate(2), partner)
+
+    def sent(leg, k):
+        if leg == 0:
+            @pl.when(s < ns - 1)
+            def _():
+                blocks(leg, k, len(DIRECT), send_sem.at[leg, k])
+
+            if len(DIRECT) > 1:
+                @pl.when(s == ns - 1)
+                def _():
+                    blocks(leg, k, len(DIRECT) - 1, send_sem.at[leg, k])
+        else:
+            @pl.when(s > 0)
+            def _():
+                blocks(leg, k, len(DIRECT), send_sem.at[leg, k])
 
     def step(leg, k):
         acc = jnp.zeros((T, hs), f32)
-
-        def arrived(b):
-            block = u.at[leg, k, b]
-            pltpu.make_async_copy(block, block, recv.at[leg, k, b]).wait()
-
-        for dy in (2, 3, 1, 0):
-            b = 2 * lax.rem(y + dy, ny) + c
-
-            def pass_on(b=b):
-                arrived(b)
-                pltpu.make_async_remote_copy(
-                    src_ref=u.at[leg, k, b],
-                    dst_ref=u.at[leg, k, b],
-                    send_sem=relay_sem.at[leg, k],
-                    recv_sem=recv.at[leg, k, b],
-                    device_id={"section": s, "dp": partner},
-                    device_id_type=MESH,
-                ).start()
-
-            if leg == 0:
-                pl.when(s > 0)(pass_on)
-            else:
-                pass_on()
-            acc += jnp.dot(u[leg, k, b][:, : 2 * hs], wt[leg, b], preferred_element_type=f32)
-        for dy in (2, 3, 1, 0):
-            b = 2 * lax.rem(y + dy, ny) + 1 - c
-            if leg == 0:
-                pl.when(s > 0)(functools.partial(arrived, b))
-            else:
-                arrived(b)
+        here = (lane_mate(0), lane_mate(2))
+        due = (other_lane(0), lane_mate(3), other_lane(3), lane_mate(1), other_lane(1), other_lane(2))
+        for n, b in enumerate(here + due):
+            if n >= len(here):
+                if leg == 0:
+                    pl.when(s > 0)(functools.partial(arrived, leg, k, b))
+                else:
+                    arrived(leg, k, b)
             acc += jnp.dot(u[leg, k, b][:, : 2 * hs], wt[leg, b], preferred_element_type=f32)
         kap = u[leg, k, 0][:, 2 * hs :].astype(f32)
         for b in range(1, nb):
@@ -278,6 +301,10 @@
         sbuf[leg, k, :, hs : 2 * hs] = new_g.astype(jnp.bfloat16)
         sbuf[leg, k, :, 2 * hs :] = jnp.broadcast_to(part, (T, 128)).astype(jnp.bfloat16)
 
+        @pl.when(k > 0)
+        def _():
+            sent(leg, k - 1)
+
         def send(section, to_leg, dys):
             for dy in dys:
                 pltpu.make_async_remote_copy(
@@ -292,19 +319,19 @@
         if leg == 0:
             @pl.when(s < ns - 1)
             def _():
-                send(s + 1, 0, (2, 1, 3, 0))
+                send(s + 1, 0, DIRECT)
 
             @pl.when(s == ns - 1)
             def _():
-                send(s, 1, (2, 1, 3))
+                send(s, 1, DIRECT[:-1])
                 pltpu.make_async_copy(sbuf.at[0, k], u.at[1, k, me], recv.at[1, k, me]).start()
         else:
             @pl.when(s > 0)
             def _():
-                send(s - 1, 1, (2, 1, 3, 0))
-
-            owner = lax.div(k, per_owner)
-            half = lax.rem(k, per_owner)
+                send(s - 1, 1, DIRECT)
+
+            owner = lax.rem(k, nb)
+            half = lax.div(k, nb)
 
             @pl.when(owner == me)
             def _():
@@ -362,35 +389,71 @@
             ).wait()
 
     stat_me[...] = jnp.zeros_like(stat_me)
-    lag = jnp.minimum(nc, LAG[0] + LAG[1] * (ns - 1 - s))
-    early = lag < nc
-    prepare_at = jnp.where(early, 0, nc)
-    grad_at = jnp.where(early, nc + lag, nc)
+    lag = jnp.minimum(nc - 1 + TAKE, LAG[0] + LAG[1] * (ns - 1 - s))
+    grad_at = jnp.where(s < GRAD, nc - 1, nc + lag)
+
+    def prepare():
+        send_slices(1)
+        send_rows(1)
+        send_scales(1)
+        for part in range(per_owner):
+            spread_rows(1, part)
+        for part in range(per_owner):
+            relay_rows(1, part)
+        transpose_weight(1)
+        local_factors(1)
+        for part in range(per_owner):
+            fill_q(1, part)
 
     def advance(i, _):
-        @pl.when(i == prepare_at)
-        def _():
-            spread_rows(1)
-            relay_rows(1)
-            transpose_weight(1)
-            local_factors(1)
-            fill_q(1)
+        j = i - lag
+
+        @pl.when((i == -TAKE) & (s >= PREPARE))
+        def _():
+            prepare()
+
+        for ahead, action in ((nb + 1, spread_rows), (5, relay_rows), (2, fill_q)):
+            k = i + ahead
+
+            @pl.when((s < LAZY) & (k >= nb) & (k < nc) & (lax.rem(k, nb) == 0))
+            def _(k=k, action=action):
+                action(0, lax.div(k, nb))
+
+        @pl.when((i + TAKE < nc) & (s > 0))
+        def _():
+            take(0, i + TAKE)
+
+        @pl.when((i >= 0) & (i < nc))
+        def _():
+            step(0, i)
+
+        @pl.when((i + TAKE < nc) & (s > 0))
+        def _():
+            relay(0, i + TAKE)
+
+        @pl.when((i == nc - 1) & (s < PREPARE))
+        def _():
+            prepare()
 
         @pl.when(i == grad_at)
         def _():
             weight_grad(0)
 
-        @pl.when(i < nc)
-        def _():
-            step(0, i)
-
-        @pl.when((i >= lag) & (i < nc + lag))
-        def _():
-            step(1, i - lag)
+        @pl.when((j + TAKE >= 0) & (j + TAKE < nc))
+        def _():
+            take(1, j + TAKE)
+
+        @pl.when((j >= 0) & (j < nc))
+        def _():
+            step(1, j)
+
+        @pl.when((j + TAKE >= 0) & (j + TAKE < nc))
+        def _():
+            relay(1, j + TAKE)
 
         return 0
 
-    lax.fori_loop(0, nc + lag + 1, advance, 0)
+    lax.fori_loop(-TAKE, nc + lag + 1, advance, 0)
     weight_grad(1)
 
     stat_dp[me] = stat_me[...]
@@ -432,27 +495,19 @@
     stats[0] = jnp.sum(both[:, 0], axis=0)
     stats[1] = jnp.max(both[:, 1], axis=0)
 
+    sent(0, nc - 1)
+    sent(1, nc - 1)
+
     def drain(k, _):
-        four = u.at[0, k, pl.ds(0, ny)]
-        three = u.at[0, k, pl.ds(0, ny - 1)]
         one = u.at[0, k, 0]
 
         @pl.when(s > 0)
         def _():
-            pltpu.make_async_copy(four, four, relay_sem.at[0, k]).wait()
-            pltpu.make_async_copy(four, four, send_sem.at[1, k]).wait()
-
-        pltpu.make_async_copy(four, four, relay_sem.at[1, k]).wait()
-
-        @pl.when(s < ns - 1)
-        def _():
-            pltpu.make_async_copy(four, four, send_sem.at[0, k]).wait()
-
-        @pl.when(s == ns - 1)
-        def _():
-            pltpu.make_async_copy(three, three, send_sem.at[0, k]).wait()
-
-        @pl.when(lax.div(k, per_owner) != me)
+            blocks(0, k, 6, relay_sem.at[0, k])
+
+        blocks(1, k, 6, relay_sem.at[1, k])
+
+        @pl.when(lax.rem(k, nb) != me)
         def _():
             pltpu.make_async_copy(one, one, own_send.at[k]).wait()
 
@@ -532,8 +587,8 @@
             dma((2,)),
             dma((2,)),
             dma((2,)),
-            dma((2, nb)),
-            dma((2,)),
+            dma((2, per_owner, nb)),
+            dma((2, per_owner)),
         ],
         compiler_params=pltpu.CompilerParams(
             collective_id=0, has_side_effects=True, vmem_limit_bytes=60 * 2**20

time: 554 us -> 491 us (0.89)
  Pallas kernels: 538 us -> 475 us
    pallas_call x1, Pallas kernels: 538 us -> 475 us  [on_device(): pl.pallas_call(functools.partial(relay_kernel, ns, nb, hs, nc), out_shape...]
where the time goes in v3:
time: 491 us
  Pallas kernels  475 us (97%)
  other arithmetic  11.5 us (2%)
    pallas_call x1, Pallas kernels, on_device(): pl.pallas_call(functools.partial(relay_kernel, ns, nb, hs, nc), out_shape...  475 us
    convert_element_type x1, other arithmetic, on_device(): weight_grads = (grads.astype(f32) * factor).astype(bf16)  10.2 us

profile of v3, /device:TPU:1, one launch (start us, length us, event | category | flops | bytes accessed | tf_op | source)
XLA Modules:
  0.0 490.9 jit_solution(3571097955370353409)
XLA Ops:
  0.6 475.4 %relay.1 = (bf16[2,1,384,6144]{3,2,1,0:T(8,128)(2,1)}, bf16[4,16,6144]{2,1,0:T(8,128)(2,1)}, f32[2,8,128]{2,1,0:T(8,128)}) custom-call(bf16[2,1,384,6144]{3,2,1,0:T(8,128)(2,1)} %w_hbm.1, bf16[2,4,16,6144]{3,2,1,0:T(8,128)(2,1)} %bitcast.2, bf16[4,16,6144]{2,1,0:T(8,128)(2,1)} %cot_hbm.1), custom_call_target="tpu_custom_call" | custom-call | tf_op jit(solution)/shard_map/relay/pallas_call | solution.py:547
  476.0 1.3 slice_reduce_fusion
  478.7 0.0 copy-start
  478.7 10.2 %multiply_convert_fusion = bf16[2,1,384,6144]{3,2,1,0:T(8,128)(2,1)} fusion(bf16[2,1,384,6144]{3,2,1,0:T(8,128)(2,1)} %get-tuple-element.7, f32[]{:T(128)S(6)} %min_shard_map.3), kind=kLoop, calls=%fused_computation | loop fusion | flops 14155776 | bytes 18874372 | tf_op jit(solution)/shard_map/convert_element_type | solution.py:607
  488.8 0.0 copy-done
  488.8 0.9 copy.7
Async XLA Ops:
  478.7 10.2 %copy-start = (bf16[4,16,6144]{2,1,0:T(8,128)(2,1)S(1)}, bf16[4,16,6144]{2,1,0:T(8,128)(2,1)}, u32[]{:S(2)}) copy-start(bf16[4,16,6144]{2,1,0:T(8,128)(2,1)} %get-tuple-element.6) | copy-start | bytes 2359300

commit v4 on v3

--- a/solution.py
+++ b/solution.py
@@ -10,12 +10,14 @@
 epsilon = 1e-05
 MESH = pl.DeviceIdType.MESH
 T = 16
-TAKE = 1
-LAG = (3, 7)
+TAKE = 2
+LAG = (4, 9)
 LAZY = 3
 PREPARE = 9
 GRAD = 4
-DIRECT = (2, 0)
+DIRECT = (0,)
+FORWARD = (2, 1, 3)
+PASS = 1
 
 
 def relay_kernel(
@@ -212,8 +214,8 @@
     def _():
         def clear(k, _):
             for b in range(nb):
-                u[0, k, b, :, : 2 * hs] = jnp.zeros((T, 2 * hs), bf16)
-                u[0, k, b, :, 2 * hs :] = jnp.full((T, 128), -1.0 if b == 0 else 0.0, bf16)
+                u[0, k, b % 2, b // 2, :, : 2 * hs] = jnp.zeros((T, 2 * hs), bf16)
+                u[0, k, b % 2, b // 2, :, 2 * hs :] = jnp.full((T, 128), -1.0 if b == 0 else 0.0, bf16)
             return 0
 
         lax.fori_loop(0, nc, clear, 0)
@@ -229,34 +231,26 @@
             relay_rows(0, part)
             fill_q(0, part)
 
-    def arrived(leg, k, b):
-        block = u.at[leg, k, b]
-        pltpu.make_async_copy(block, block, recv.at[leg, k, b]).wait()
-
-    def pass_on(leg, k, b, dp):
-        block = u.at[leg, k, b]
-        remote(block, block, relay_sem.at[leg, k], recv.at[leg, k, b], s, dp).start()
-
-    def lane_mate(dy):
-        return 2 * lax.rem(y + dy, ny) + c
-
-    def other_lane(dy):
-        return lane_mate(dy) + 1 - 2 * c
+    def arrived(some, leg, k, which):
+        pltpu.make_async_copy(some, some, recv.at[leg, k, which]).wait()
 
     def blocks(leg, k, count, semaphore):
-        some = u.at[leg, k, pl.ds(0, count)]
+        some = u.at[leg, k, 0, pl.ds(0, count)]
         pltpu.make_async_copy(some, some, semaphore).wait()
 
     def take(leg, k):
-        arrived(leg, k, me)
-        for dy in (1, 3):
-            for mate in (lane_mate(dy), other_lane(dy)):
-                pass_on(leg, k, me, mate)
-        pass_on(leg, k, me, partner)
+        block = u.at[leg, k, c, y]
+        arrived(block, leg, k, 0)
+        for dy in FORWARD:
+            dp = 2 * lax.rem(y + dy, ny) + c
+            remote(block, block, relay_sem.at[leg, k], recv.at[leg, k, 2], s, dp).start()
 
     def relay(leg, k):
-        arrived(leg, k, lane_mate(2))
-        pass_on(leg, k, lane_mate(2), partner)
+        arrived(u.at[leg, k, 0, pl.ds(0, ny - 1)], leg, k, 2)
+        lane_blocks = u.at[leg, k, c]
+        remote(
+            lane_blocks, lane_blocks, relay_sem.at[leg, k], recv.at[leg, k, 1], s, partner
+        ).start()
 
     def sent(leg, k):
         if leg == 0:
@@ -275,21 +269,23 @@
 
     def step(leg, k):
         acc = jnp.zeros((T, hs), f32)
-        here = (lane_mate(0), lane_mate(2))
-        due = (other_lane(0), lane_mate(3), other_lane(3), lane_mate(1), other_lane(1), other_lane(2))
-        for n, b in enumerate(here + due):
-            if n >= len(here):
+        kap = jnp.zeros((T, 128), f32)
+        for which, lane in enumerate((c, 1 - c)):
+            if which == 1:
+                all_four = functools.partial(arrived, u.at[leg, k, lane], leg, k, 1)
                 if leg == 0:
-                    pl.when(s > 0)(functools.partial(arrived, leg, k, b))
+                    pl.when(s > 0)(all_four)
                 else:
-                    arrived(leg, k, b)
-            acc += jnp.dot(u[leg, k, b][:, : 2 * hs], wt[leg, b], preferred_element_type=f32)
-        kap = u[leg, k, 0][:, 2 * hs :].astype(f32)
-        for b in range(1, nb):
-            kap += u[leg, k, b][:, 2 * hs :].astype(f32)
+                    all_four()
+            for row in range(ny):
+                block = u[leg, k, lane, row]
+                acc += jnp.dot(
+                    block[:, : 2 * hs], wt[leg, 2 * row + lane], preferred_element_type=f32
+                )
+                kap += block[:, 2 * hs :].astype(f32)
         kap = jnp.concatenate([kap] * (hs // 128), axis=1)
         dh = acc - kap * q[leg, k]
-        mine = u[leg, k, me].astype(f32)
+        mine = u[leg, k, c, y].astype(f32)
         x_mine = [
             xg[leg, k, :, pl.ds(pl.multiple_of(part * half_width + me * hs, 128), hs)].astype(f32)
             for part in range(2)
@@ -301,17 +297,13 @@
         sbuf[leg, k, :, hs : 2 * hs] = new_g.astype(jnp.bfloat16)
         sbuf[leg, k, :, 2 * hs :] = jnp.broadcast_to(part, (T, 128)).astype(jnp.bfloat16)
 
-        @pl.when(k > 0)
-        def _():
-            sent(leg, k - 1)
-
         def send(section, to_leg, dys):
             for dy in dys:
                 pltpu.make_async_remote_copy(
                     src_ref=sbuf.at[leg, k],
-                    dst_ref=u.at[to_leg, k, me],
+                    dst_ref=u.at[to_leg, k, c, y],
                     send_sem=send_sem.at[leg, k],
-                    recv_sem=recv.at[to_leg, k, me],
+                    recv_sem=recv.at[to_leg, k, 0 if dy == 0 else 2],
                     device_id={"section": section, "dp": 2 * lax.rem(y + dy, ny) + c},
                     device_id_type=MESH,
                 ).start()
@@ -324,7 +316,7 @@
             @pl.when(s == ns - 1)
             def _():
                 send(s, 1, DIRECT[:-1])
-                pltpu.make_async_copy(sbuf.at[0, k], u.at[1, k, me], recv.at[1, k, me]).start()
+                pltpu.make_async_copy(sbuf.at[0, k], u.at[1, k, c, y], recv.at[1, k, 0]).start()
         else:
             @pl.when(s > 0)
             def _():
@@ -352,7 +344,7 @@
 
         for b in range(nb):
             for part in range(2):
-                value = u[leg, k, b, :, part * hs : (part + 1) * hs].astype(f32)
+                value = u[leg, k, b % 2, b // 2, :, part * hs : (part + 1) * hs].astype(f32)
                 value -= kap * xg[leg, k, :, columns_of(b, part)].astype(f32)
                 xg[leg, k, :, columns_of(b, part)] = value.astype(bf16)
 
@@ -425,11 +417,14 @@
 
         @pl.when((i >= 0) & (i < nc))
         def _():
+            if PASS == 0:
+                pl.when(s > 0)(functools.partial(relay, 0, i))
             step(0, i)
 
-        @pl.when((i + TAKE < nc) & (s > 0))
-        def _():
-            relay(0, i + TAKE)
+        if PASS == 1:
+            @pl.when((i + 1 >= 0) & (i + 1 < nc) & (s > 0))
+            def _():
+                relay(0, i + 1)
 
         @pl.when((i == nc - 1) & (s < PREPARE))
         def _():
@@ -445,11 +440,14 @@
 
         @pl.when((j >= 0) & (j < nc))
         def _():
+            if PASS == 0:
+                relay(1, j)
             step(1, j)
 
-        @pl.when((j + TAKE >= 0) & (j + TAKE < nc))
-        def _():
-            relay(1, j + TAKE)
+        if PASS == 1:
+            @pl.when((j + 1 >= 0) & (j + 1 < nc))
+            def _():
+                relay(1, j + 1)
 
         return 0
 
@@ -495,17 +493,20 @@
     stats[0] = jnp.sum(both[:, 0], axis=0)
     stats[1] = jnp.max(both[:, 1], axis=0)
 
-    sent(0, nc - 1)
-    sent(1, nc - 1)
+    def drained(leg, k):
+        some = obuf.at[0, pl.ds(0, ny + len(FORWARD))]
+        pltpu.make_async_copy(some, some, relay_sem.at[leg, k]).wait()
 
     def drain(k, _):
-        one = u.at[0, k, 0]
+        one = u.at[0, k, 0, 0]
+        sent(0, k)
+        sent(1, k)
 
         @pl.when(s > 0)
         def _():
-            blocks(0, k, 6, relay_sem.at[0, k])
-
-        blocks(1, k, 6, relay_sem.at[1, k])
+            drained(0, k)
+
+        drained(1, k)
 
         @pl.when(lax.rem(k, nb) != me)
         def _():
@@ -529,6 +530,10 @@
     @pl.when(s > 0)
     def _():
         pltpu.make_async_copy(one, one, hop_send.at[1]).wait()
+
+
+def scale_kernel(factor, grads, scaled):
+    scaled[...] = (grads[...].astype(jnp.float32) * factor[0]).astype(jnp.bfloat16)
 
 
 def on_device(cotangent, saved_inputs, weights):
@@ -540,6 +545,7 @@
     per_owner = rows // T
     nc = per_owner * nb
     wide = 2 * hs + 128
+    ny = nb // 2
 
     vmem = pl.BlockSpec(memory_space=pltpu.VMEM)
     hbm = pl.BlockSpec(memory_space=pl.ANY)
@@ -556,7 +562,7 @@
         scratch_shapes=[
             pltpu.VMEM((2, nb, 2 * hs, hs), bf16),
             pltpu.VMEM((2, nc, T, width), bf16),
-            pltpu.VMEM((2, nc, nb, T, wide), bf16),
+            pltpu.VMEM((2, nc, 2, ny, T, wide), bf16),
             pltpu.VMEM((2, nc, T, hs), f32),
             pltpu.VMEM((2, 3, nc, T, hs), f32),
             pltpu.VMEM((2, nc, T, hs), bf16),
@@ -571,7 +577,7 @@
             pltpu.VMEM((nb, 2, 8, 128), f32),
             pltpu.VMEM((ns, 2, 8, 128), f32),
             pltpu.VMEM((2, 8, 128), f32),
-            dma((2, nc, nb)),
+            dma((2, nc, 3)),
             dma((2, nc)),
             dma((2, nc)),
             dma((nc,)),
@@ -604,7 +610,15 @@
     largest = jnp.max(stats[1])
     limit = 0.5 * jnp.sqrt(jnp.float32(2 * ns * (width // 2) * width))
     factor = jnp.minimum(jnp.float32(1.0), limit / jnp.sqrt(total))
-    weight_grads = (grads.astype(f32) * factor).astype(bf16)
+    piece = pl.BlockSpec((1, 1, hs // 6, width), lambda leg, i: (leg, 0, i, 0))
+    weight_grads = pl.pallas_call(
+        scale_kernel,
+        grid=(2, 6),
+        out_shape=jax.ShapeDtypeStruct(grads.shape, bf16),
+        in_specs=[pl.BlockSpec(memory_space=pltpu.SMEM), piece],
+        out_specs=piece,
+        name="scale",
+    )(factor.reshape(1), grads)
     return (leaving.reshape(1, *cotangent.shape), weight_grads, factor * largest)
 
 

time: 491 us -> 467 us (0.951)
  Pallas kernels: 475 us -> 461 us
  other arithmetic: 11.5 us -> 1.3 us
    pallas_call x1, Pallas kernels: 475 us -> 449 us  [on_device(): pl.pallas_call(functools.partial(relay_kernel, ns, nb, hs, nc), out_shape...]
    pallas_call x0 -> x1, Pallas kernels: none -> 11.9 us  [on_device(): pl.pallas_call(scale_kernel, grid=(2, 6), out_shape=jax.ShapeDtypeStruct(...]
    convert_element_type x1 -> x0, other arithmetic: 10.2 us -> none  [on_device(): weight_grads = (grads.astype(f32) * factor).astype(bf16)]
where the time goes in v4:
time: 467 us; the launch traced here: 466 us
  Pallas kernels  461 us (99%)
    pallas_call x1, Pallas kernels, on_device(): pl.pallas_call(functools.partial(relay_kernel, ns, nb, hs, nc), out_shape...  449 us
    pallas_call x1, Pallas kernels, on_device(): pl.pallas_call(scale_kernel, grid=(2, 6), out_shape=jax.ShapeDtypeStruct(...  11.9 us

profile of v4, /device:TPU:1, one launch (start us, length us, event | category | flops | bytes accessed | tf_op | source)
XLA Modules:
  0.0 466.4 jit_solution(4819248234916919642)
XLA Ops:
  0.6 449.2 %relay.1 = (bf16[2,1,384,6144]{3,2,1,0:T(8,128)(2,1)}, bf16[4,16,6144]{2,1,0:T(8,128)(2,1)}, f32[2,8,128]{2,1,0:T(8,128)}) custom-call(bf16[2,1,384,6144]{3,2,1,0:T(8,128)(2,1)} %w_hbm.1, bf16[2,4,16,6144]{3,2,1,0:T(8,128)(2,1)} %bitcast.3, bf16[4,16,6144]{2,1,0:T(8,128)(2,1)} %cot_hbm.1), custom_call_target="tpu_custom_call" | custom-call | tf_op jit(solution)/shard_map/relay/pallas_call | solution.py:553
  449.8 1.3 slice_reduce_fusion
  452.4 0.0 copy-start
  452.4 11.9 %scale.1 = bf16[2,1,384,6144]{3,2,1,0:T(8,128)(2,1)} custom-call(f32[1]{0:T(128)} %bitcast.2.factor, bf16[2,1,384,6144]{3,2,1,0:T(8,128)(2,1)} %get-tuple-element.8.grads), custom_call_target="tpu_custom_call" | custom-call | tf_op jit(solution)/shard_map/scale/pallas_call | solution.py:614
  464.4 0.0 copy-done
  464.4 0.9 copy.7
Async XLA Ops:
  452.4 12.0 %copy-start = (bf16[4,16,6144]{2,1,0:T(8,128)(2,1)S(1)}, bf16[4,16,6144]{2,1,0:T(8,128)(2,1)}, u32[]{:S(2)}) copy-start(bf16[4,16,6144]{2,1,0:T(8,128)(2,1)} %get-tuple-element.6) | copy-start | bytes 2359300

commit v5 on v4

--- a/solution.py
+++ b/solution.py
@@ -13,7 +13,8 @@
 TAKE = 2
 LAG = (4, 9)
 LAZY = 3
-PREPARE = 9
+PREPARE = 10
+AHEAD = 8
 GRAD = 4
 DIRECT = (0,)
 FORWARD = (2, 1, 3)
@@ -384,12 +385,21 @@
     lag = jnp.minimum(nc - 1 + TAKE, LAG[0] + LAG[1] * (ns - 1 - s))
     grad_at = jnp.where(s < GRAD, nc - 1, nc + lag)
 
-    def prepare():
+    def fetch():
         send_slices(1)
         send_rows(1)
         send_scales(1)
+
+    def spread():
         for part in range(per_owner):
             spread_rows(1, part)
+
+    def prepare():
+        @pl.when((s < AHEAD) | (s >= PREPARE))
+        def _():
+            fetch()
+            spread()
+
         for part in range(per_owner):
             relay_rows(1, part)
         transpose_weight(1)
@@ -425,6 +435,10 @@
             @pl.when((i + 1 >= 0) & (i + 1 < nc) & (s > 0))
             def _():
                 relay(0, i + 1)
+
+        between = (s >= AHEAD) & (s < PREPARE)
+        pl.when((i == nc // 4) & between)(fetch)
+        pl.when((i == nc - nc // 4) & between)(spread)
 
         @pl.when((i == nc - 1) & (s < PREPARE))
         def _():
@@ -530,10 +544,6 @@
     @pl.when(s > 0)
     def _():
         pltpu.make_async_copy(one, one, hop_send.at[1]).wait()
-
-
-def scale_kernel(factor, grads, scaled):
-    scaled[...] = (grads[...].astype(jnp.float32) * factor[0]).astype(jnp.bfloat16)
 
 
 def on_device(cotangent, saved_inputs, weights):
@@ -610,15 +620,7 @@
     largest = jnp.max(stats[1])
     limit = 0.5 * jnp.sqrt(jnp.float32(2 * ns * (width // 2) * width))
     factor = jnp.minimum(jnp.float32(1.0), limit / jnp.sqrt(total))
-    piece = pl.BlockSpec((1, 1, hs // 6, width), lambda leg, i: (leg, 0, i, 0))
-    weight_grads = pl.pallas_call(
-        scale_kernel,
-        grid=(2, 6),
-        out_shape=jax.ShapeDtypeStruct(grads.shape, bf16),
-        in_specs=[pl.BlockSpec(memory_space=pltpu.SMEM), piece],
-        out_specs=piece,
-        name="scale",
-    )(factor.reshape(1), grads)
+    weight_grads = (grads.astype(f32) * factor).astype(bf16)
     return (leaving.reshape(1, *cotangent.shape), weight_grads, factor * largest)
 
 

time: 467 us -> 498 us (1.066)
  Pallas kernels: 461 us -> 482 us
  other arithmetic: 1.3 us -> 11.5 us
    pallas_call x1, Pallas kernels: 449 us -> 482 us  [on_device(): pl.pallas_call(functools.partial(relay_kernel, ns, nb, hs, nc), out_shape...]
    pallas_call x1 -> x0, Pallas kernels: 11.9 us -> none  [on_device(): pl.pallas_call(scale_kernel, grid=(2, 6), out_shape=jax.ShapeDtypeStruct(...]
    convert_element_type x0 -> x1, other arithmetic: none -> 10.2 us  [on_device(): weight_grads = (grads.astype(f32) * factor).astype(bf16)]
where the time goes in v5:
time: 498 us
  Pallas kernels  482 us (97%)
  other arithmetic  11.5 us (2%)
    pallas_call x1, Pallas kernels, on_device(): pl.pallas_call(functools.partial(relay_kernel, ns, nb, hs, nc), out_shape...  482 us
    convert_element_type x1, other arithmetic, on_device(): weight_grads = (grads.astype(f32) * factor).astype(bf16)  10.2 us

profile of v5, /device:TPU:1, one launch (start us, length us, event | category | flops | bytes accessed | tf_op | source)
XLA Modules:
  0.0 497.6 jit_solution(904257733154557561)
XLA Ops:
  0.6 482.2 %relay.1 = (bf16[2,1,384,6144]{3,2,1,0:T(8,128)(2,1)}, bf16[4,16,6144]{2,1,0:T(8,128)(2,1)}, f32[2,8,128]{2,1,0:T(8,128)}) custom-call(bf16[2,1,384,6144]{3,2,1,0:T(8,128)(2,1)} %w_hbm.1, bf16[2,4,16,6144]{3,2,1,0:T(8,128)(2,1)} %bitcast.2, bf16[4,16,6144]{2,1,0:T(8,128)(2,1)} %cot_hbm.1), custom_call_target="tpu_custom_call" | custom-call | tf_op jit(solution)/shard_map/relay/pallas_call | solution.py:563
  482.8 1.3 slice_reduce_fusion
  485.4 0.0 copy-start
  485.5 10.2 %multiply_convert_fusion = bf16[2,1,384,6144]{3,2,1,0:T(8,128)(2,1)} fusion(bf16[2,1,384,6144]{3,2,1,0:T(8,128)(2,1)} %get-tuple-element.7, f32[]{:T(128)S(6)} %min_shard_map.3), kind=kLoop, calls=%fused_computation | loop fusion | flops 14155776 | bytes 18874372 | tf_op jit(solution)/shard_map/convert_element_type | solution.py:623
  495.6 0.0 copy-done
  495.6 0.9 copy.7
Async XLA Ops:
  485.4 10.2 %copy-start = (bf16[4,16,6144]{2,1,0:T(8,128)(2,1)S(1)}, bf16[4,16,6144]{2,1,0:T(8,128)(2,1)}, u32[]{:S(2)}) copy-start(bf16[4,16,6144]{2,1,0:T(8,128)(2,1)} %get-tuple-element.6) | copy-start | bytes 2359300
